TPU v7x, 128 devices: a whole 4x4x4 slice. The times are simulated.
128 devices in a mesh: dp: 8 (over x, core), ctx: 4 (over y), tp: 4 (over z).
Axes of the slice: x: 4, y: 4, z: 4, core: 2. Of those that a mesh axis runs over, the one named last changes fastest.
Arguments:
- tokens: float32 [8192, 2048], P(('dp', 'ctx')), may hold values from -6 to 6
- cotangent: float32 [8192, 2048], P(('dp', 'ctx')), may hold values from -6 to 6
- gain_first: float32 [2048], replicated, may hold values from 0.25 to 1.75
- gain_second: float32 [2048], replicated, may hold values from 0.25 to 1.75
- w_query: bfloat16 [2048, 2048], P(('dp', 'ctx'), 'tp'), may hold values from -0.125 to 0.125
- w_key: bfloat16 [2048, 2048], P(('dp', 'ctx'), 'tp'), may hold values from -0.125 to 0.125
- w_value: bfloat16 [2048, 4096], P(('dp', 'ctx'), 'tp'), may hold values from -0.125 to 0.125
- w_gate: bfloat16 [2048, 4096], P(('dp', 'ctx'), 'tp'), may hold values from -0.125 to 0.125
- w_output: bfloat16 [4096, 2048], P('tp', ('dp', 'ctx')), may hold values from -0.125 to 0.125
- w_hidden: bfloat16 [2048, 4096], P(('dp', 'ctx'), 'tp'), may hold values from -0.125 to 0.125
- w_linear: bfloat16 [2048, 4096], P(('dp', 'ctx'), 'tp'), may hold values from -0.125 to 0.125
- w_down: bfloat16 [4096, 2048], P('tp', ('dp', 'ctx')), may hold values from -0.125 to 0.125
- decay_scale: float32 [8], P('tp'), may hold values from 0.3 to 40
- first_length: int32 [8], P('dp'), may hold values from 769 to 1024, as said below
Outputs:
- layer_out: float32 [8192, 2048], P(('dp', 'ctx'))
- input_grad: float32 [8192, 2048], P(('dp', 'ctx'))
- gain_first_grad: float32 [2048], P(('dp', 'ctx'))
- gain_second_grad: float32 [2048], P(('dp', 'ctx'))
- query_grad: float32 [2048, 2048], P(('dp', 'ctx'), 'tp')
- key_grad: float32 [2048, 2048], P(('dp', 'ctx'), 'tp')
- value_grad: float32 [2048, 4096], P(('dp', 'ctx'), 'tp')
- gate_grad: float32 [2048, 4096], P(('dp', 'ctx'), 'tp')
- output_grad: float32 [4096, 2048], P('tp', ('dp', 'ctx'))
- hidden_grad: float32 [2048, 4096], P(('dp', 'ctx'), 'tp')
- linear_grad: float32 [2048, 4096], P(('dp', 'ctx'), 'tp')
- down_grad: float32 [4096, 2048], P('tp', ('dp', 'ctx'))
Inputs may be any that keep to these rules, and one draw needn't show every extreme that they name: Rows of group g after the first first_length[g] form a second sequence; in some group it is empty.
All inputs are finite; a program needn't handle non-finite values.
Results may differ from a plain program's by a relative error of at most 0.03.
Values may be sent and summed in bfloat16 or wider, within the bound.
No kernel may reach another device: no remote copies, remote signals or barrier semaphores. Data moves between devices by JAX's collectives and lax.ppermute only.
A program may use at most 128 MiB of HBM per device.

v0:
```python
import jax
import jax.numpy as jnp
from jax import lax
from jax.sharding import PartitionSpec as P

DK = 256
DV = 512


precise = lax.Precision.HIGHEST


def prefix(x, axis, combine, identity):
    count, index = (lax.axis_size(axis), lax.axis_index(axis))
    everything = jax.tree.map(
        lambda part, kind: lax.all_gather(part.astype(kind), axis), x, (jnp.bfloat16, jnp.bfloat16)
    )
    start = jax.tree.map(
        lambda part, zero: jnp.broadcast_to(jnp.asarray(zero, part.dtype), part.shape), x, identity
    )

    def hop(k, before):
        reached = k < index
        new = combine(
            before, jax.tree.map(lambda part, own: part[k].astype(own.dtype), everything, x)
        )
        return jax.tree.map(lambda a, b: jnp.where(reached, a, b), new, before)

    return lax.fori_loop(0, count, hop, start)


def carried_in(x, axis, join, neutral):
    count = lax.axis_size(axis)
    place = lax.axis_index(axis)
    ahead = count - 1 - place
    gathered = jax.tree.map(
        lambda a, kind: lax.all_gather(a.astype(kind), axis),
        x,
        jax.tree.map(lambda a: jnp.bfloat16 if a.dtype == jnp.float32 else a.dtype, x),
    )
    state = jax.tree.map(lambda a, e: jnp.zeros_like(a) + jnp.asarray(e, a.dtype), x, neutral)

    def one(hop, state):
        source = count - 1 - hop
        return join(
            state,
            jax.tree.map(
                lambda a, own: lax.dynamic_index_in_dim(a, source, 0, False).astype(own.dtype),
                gathered,
                x,
            ),
        )

    return lax.fori_loop(0, ahead, one, state)


def mean_scale(values, gain):
    factor = lax.rsqrt(jnp.mean(values * values, axis=-1, keepdims=True) + 1e-06)
    return values * factor * gain


def gate_norm(gate_pre, retained):
    row_count = retained.shape[0]
    grouped = retained.reshape(row_count, -1, DV)
    centred = grouped - jnp.mean(grouped, axis=-1, keepdims=True)
    normed = centred * lax.rsqrt(jnp.mean(centred * centred, axis=-1, keepdims=True) + 1.0 * DK)
    return gate_pre * jax.nn.sigmoid(gate_pre) * normed.reshape(row_count, -1)


def gelu_gate(hidden, linear):
    return jax.nn.gelu(hidden, approximate=True) * linear


def rotate(values, positions, direction):
    half = DK // 2
    frequency = 10000.0 ** (-(jnp.arange(half).astype(values.dtype) / half))
    angles = positions[:, None] * frequency[None, :]
    cosine = jnp.cos(angles)[:, None, :]
    sine = jnp.sin(angles)[:, None, :] * direction
    shaped = values.reshape(values.shape[0], -1, DK)
    first = shaped[..., :half]
    second = shaped[..., half:]
    turned = jnp.concatenate(
        (first * cosine - second * sine, first * sine + second * cosine), axis=-1
    )
    return turned.reshape(values.shape)


def times_transposed(left, right):
    return lax.dot_general(
        left, right, (((1,), (1,)), ((), ())), preferred_element_type=jnp.float32
    )


def transposed_times(left, right):
    return lax.dot_general(
        left, right, (((0,), (0,)), ((), ())), preferred_element_type=jnp.float32
    )


def chain(earlier, later):
    return (earlier[0] * later[0], later[0][:, None, None] * earlier[1] + later[1])


def heads_total(partial_sum):
    return lax.psum(partial_sum.astype(jnp.bfloat16), "tp").astype(jnp.float32)


def send_rows(members):
    return (
        lax.psum_scatter(
            members[0].astype(jnp.bfloat16), ("dp", "ctx"), scatter_dimension=0, tiled=True
        ).astype(jnp.float32),
        lax.psum_scatter(
            members[1].astype(jnp.bfloat16), ("dp", "ctx"), scatter_dimension=0, tiled=True
        ).astype(jnp.float32),
    )


def send_cols(member):
    return lax.psum_scatter(
        member.astype(jnp.bfloat16), ("dp", "ctx"), scatter_dimension=1, tiled=True
    ).astype(jnp.float32)


def retention_forward(query_rot, key_rot, value_low, rates, carried, at_end, document, local_index):
    tok_rows = query_rot.shape[0]
    heads_here = rates.shape[0]
    query_heads = query_rot.reshape(tok_rows, heads_here, DK)
    key_heads = key_rot.reshape(tok_rows, heads_here, DK)
    value_full = value_low.reshape(tok_rows, heads_here, DV).astype(jnp.float32)
    query_full = query_heads.astype(jnp.float32)
    key_full = key_heads.astype(jnp.float32)
    offsets = local_index[:, None] - local_index[None, :]
    linked = (offsets >= 0) & (document[:, None] == document[None, :])
    decays = jnp.exp(-rates[:, None, None] * jnp.maximum(offsets, 0).astype(jnp.float32)[None])
    mask = jnp.where(linked[None], decays, 0.0)
    scores = jnp.einsum("ihd,jhd->hij", query_heads, key_heads, preferred_element_type=jnp.float32)
    weighted = scores * mask
    inner = jnp.einsum("hij,jhe->ihe", weighted, value_full, precision=precise)
    steps = local_index.astype(jnp.float32)
    enter = carried[:, None] * jnp.exp(-rates[None, :] * (steps[:, None] + 1.0))
    leave = at_end[:, None] * jnp.exp(-rates[None, :] * (tok_rows - 1.0 - steps)[:, None])
    through = jnp.exp(-rates * tok_rows) * carried[tok_rows - 1]
    local_state = jnp.einsum("jh,jhd,jhe->hde", leave, key_full, value_full, precision=precise)
    identity = (jnp.ones_like(through), jnp.zeros_like(local_state))
    prior = prefix((through, local_state), "ctx", chain, identity)
    state_in = prior[1]
    cross = jnp.einsum("ihd,hde->ihe", query_full, state_in, precision=precise) * enter[:, :, None]
    retained = (inner + cross).reshape(tok_rows, heads_here * DV)
    return (retained, (mask, weighted, state_in, enter, leave, through))


def retention_backward(grad_retained, query_rot, key_rot, value_low, saved):
    mask, weighted, state_in, enter, leave, through = saved
    tok_rows = query_rot.shape[0]
    heads_here = through.shape[0]
    query_full = query_rot.reshape(tok_rows, heads_here, DK).astype(jnp.float32)
    key_full = key_rot.reshape(tok_rows, heads_here, DK).astype(jnp.float32)
    value_full = value_low.reshape(tok_rows, heads_here, DV).astype(jnp.float32)
    grad_heads = grad_retained.reshape(tok_rows, heads_here, DV)
    grad_weighted = jnp.einsum("ihe,jhe->hij", grad_heads, value_full, precision=precise)
    grad_value = jnp.einsum("hij,ihe->jhe", weighted, grad_heads, precision=precise)
    grad_scores = grad_weighted * mask
    grad_query = jnp.einsum("hij,jhd->ihd", grad_scores, key_full, precision=precise)
    grad_query = grad_query + enter[:, :, None] * jnp.einsum(
        "ihe,hde->ihd", grad_heads, state_in, precision=precise
    )
    grad_key = jnp.einsum("hij,ihd->jhd", grad_scores, query_full, precision=precise)
    local_back = jnp.einsum("ih,ihd,ihe->hde", enter, query_full, grad_heads, precision=precise)
    identity = (jnp.ones_like(through), jnp.zeros_like(local_back))
    later = carried_in((through, local_back), "ctx", chain, identity)
    state_back = later[1]
    grad_key = grad_key + leave[:, :, None] * jnp.einsum(
        "hde,jhe->jhd", state_back, value_full, precision=precise
    )
    grad_value = grad_value + leave[:, :, None] * jnp.einsum(
        "hde,jhd->jhe", state_back, key_full, precision=precise
    )
    return (
        grad_query.reshape(tok_rows, heads_here * DK),
        grad_key.reshape(tok_rows, heads_here * DK),
        grad_value.reshape(tok_rows, heads_here * DV),
    )


def per_device(
    tokens,
    cotangent,
    gain_first,
    gain_second,
    w_query,
    w_key,
    w_value,
    w_gate,
    w_output,
    w_hidden,
    w_linear,
    w_down,
    decay_scale,
    first_length,
):
    tok_rows = tokens.shape[0]
    place = lax.axis_index("ctx")
    rates = decay_scale / (tok_rows * lax.axis_size("ctx"))
    local_index = jnp.arange(tok_rows, dtype=jnp.int32)
    global_index = place * tok_rows + local_index
    length = first_length[0]
    document = (global_index >= length).astype(jnp.int32)
    before = (place * tok_rows - 1 >= length).astype(jnp.int32)
    carried = (document == before).astype(jnp.float32)
    at_end = (document == document[tok_rows - 1]).astype(jnp.float32)
    positions = global_index.astype(jnp.float32)
    attn_in = jnp.concatenate((w_query, w_key, w_value, w_gate), axis=1)
    mlp_in = jnp.concatenate((w_hidden, w_linear), axis=1)
    local_in = (attn_in, mlp_in)
    local_out = (w_output, w_down)

    def project_in(left, pick):
        weight = local_in[pick]
        return jnp.dot(
            left,
            lax.all_gather(weight, ("dp", "ctx"), axis=0, tiled=True),
            preferred_element_type=jnp.float32,
        )

    def project_out(left, pick):
        return jnp.dot(
            left,
            lax.all_gather(local_out[pick], ("dp", "ctx"), axis=1, tiled=True),
            preferred_element_type=jnp.float32,
        )

    def back_out(grad, pick):
        weight = local_out[pick]
        return times_transposed(grad, lax.all_gather(weight, ("dp", "ctx"), axis=1, tiled=True))

    def back_in(grad, pick):
        weight = local_in[pick]
        return times_transposed(grad, lax.all_gather(weight, ("dp", "ctx"), axis=0, tiled=True))

    normed_first, first_back = jax.vjp(mean_scale, tokens, gain_first)
    low_first = normed_first.astype(jnp.bfloat16)
    projected = project_in(low_first, 0)
    key_cols = w_query.shape[1]
    value_cols = w_value.shape[1]
    query = projected[:, :key_cols]
    key_proj = projected[:, key_cols : 2 * key_cols]
    value_low = projected[:, 2 * key_cols : 2 * key_cols + value_cols].astype(jnp.bfloat16)
    gate_pre = projected[:, 2 * key_cols + value_cols :]
    query_rot = rotate(query, positions, 1.0).astype(jnp.bfloat16)
    key_rot = rotate(key_proj, positions, 1.0).astype(jnp.bfloat16)
    retained, saved = retention_forward(
        query_rot, key_rot, value_low, rates, carried, at_end, document, local_index
    )
    mixed_full, gate_back = jax.vjp(gate_norm, gate_pre, retained)
    mixed = mixed_full.astype(jnp.bfloat16)
    hidden_state = tokens + heads_total(project_out(mixed, 0))
    normed_second, second_back = jax.vjp(mean_scale, hidden_state, gain_second)
    low_second = normed_second.astype(jnp.bfloat16)
    paired = project_in(low_second, 1)
    ff_cols = w_hidden.shape[1]
    activated_full, gelu_back = jax.vjp(gelu_gate, paired[:, :ff_cols], paired[:, ff_cols:])
    activated = activated_full.astype(jnp.bfloat16)
    layer_out = hidden_state + heads_total(project_out(activated, 1))
    grad_out_low = cotangent.astype(jnp.bfloat16)
    grad_activated = back_out(grad_out_low, 1)
    grad_hidden, grad_linear = gelu_back(grad_activated)
    grad_pair = jnp.concatenate((grad_hidden, grad_linear), axis=1).astype(jnp.bfloat16)
    weight_mlp = transposed_times(low_second, grad_pair)
    weight_down = transposed_times(activated, grad_out_low)
    grad_second = heads_total(back_in(grad_pair, 1))
    grad_state_part, gain_second_part = second_back(grad_second)
    grad_state = cotangent + grad_state_part
    grad_state_low = grad_state.astype(jnp.bfloat16)
    grad_mixed = back_out(grad_state_low, 0)
    weight_output = transposed_times(mixed, grad_state_low)
    grad_gate, grad_retained = gate_back(grad_mixed)
    grad_query_rot, grad_key_rot, grad_value = retention_backward(
        grad_retained, query_rot, key_rot, value_low, saved
    )
    grad_query = rotate(grad_query_rot, positions, -1.0)
    grad_key = rotate(grad_key_rot, positions, -1.0)
    grad_proj = jnp.concatenate((grad_query, grad_key, grad_value, grad_gate), axis=1).astype(
        jnp.bfloat16
    )
    weight_attn = transposed_times(low_first, grad_proj)
    grad_first = heads_total(back_in(grad_proj, 0))
    grad_token_part, gain_first_part = first_back(grad_first)
    input_grad = grad_state + grad_token_part
    attn_sum, first_sum = send_rows((weight_attn, gain_first_part))
    mlp_sum, second_sum = send_rows((weight_mlp, gain_second_part))
    output_sum = send_cols(weight_output)
    down_sum = send_cols(weight_down)
    value_end = 2 * key_cols + value_cols
    return (
        layer_out,
        input_grad,
        first_sum,
        second_sum,
        attn_sum[:, :key_cols],
        attn_sum[:, key_cols : 2 * key_cols],
        attn_sum[:, 2 * key_cols : value_end],
        attn_sum[:, value_end:],
        output_sum,
        mlp_sum[:, :ff_cols],
        mlp_sum[:, ff_cols:],
        down_sum,
    )


def solution(mesh):
    in_specs = (
        P(("dp", "ctx"), None),
        P(("dp", "ctx"), None),
        P(),
        P(),
        P(("dp", "ctx"), "tp"),
        P(("dp", "ctx"), "tp"),
        P(("dp", "ctx"), "tp"),
        P(("dp", "ctx"), "tp"),
        P("tp", ("dp", "ctx")),
        P(("dp", "ctx"), "tp"),
        P(("dp", "ctx"), "tp"),
        P("tp", ("dp", "ctx")),
        P("tp"),
        P("dp"),
    )
    out_specs = (
        P(("dp", "ctx"), None),
        P(("dp", "ctx"), None),
        P(("dp", "ctx")),
        P(("dp", "ctx")),
        P(("dp", "ctx"), "tp"),
        P(("dp", "ctx"), "tp"),
        P(("dp", "ctx"), "tp"),
        P(("dp", "ctx"), "tp"),
        P("tp", ("dp", "ctx")),
        P(("dp", "ctx"), "tp"),
        P(("dp", "ctx"), "tp"),
        P("tp", ("dp", "ctx")),
    )
    return jax.shard_map(
        per_device, mesh=mesh, in_specs=in_specs, out_specs=out_specs, check_vma=False
    )
```

profile of v0, /device:TPU:1, one launch (start us, length us, event | category | flops | bytes accessed | tf_op | source)
XLA Modules:
  0.0 873.2 jit_solution(8693606430680210560)
XLA Ops:
  7.3 1.9 pad_maximum_fusion.4
  11.8 1.8 multiply_reduce_fusion.1
  14.4 1.2 broadcast_multiply_fusion
  15.6 61.7 %all-gather.10.cloned.1.call-done = bf16[2048,3072]{1,0:T(8,128)(2,1)} async-done(((bf16[64,3072]{1,0:T(8,128)(2,1)}), bf16[2048,3072]{1,0:T(8,128)(2,1)}) %all-gather.10.cloned.1.call-update) | async-done | bytes 12582928 | tf_op jit(solution)/shard_map/all_gather | solution.py:223
  77.4 6.5 fusion.70
  84.0 1.5 copy-done.18
  86.9 1.5 convolution_convert_fusion.8
  90.7 8.1 all-reduce
  99.4 19.2 %all-gather.18.cloned.1.call-done = bf16[8,256,512]{2,1,0:T(8,128)(2,1)} async-done(((bf16[2,256,512]{2,1,0:T(8,128)(2,1)}), bf16[8,256,512]{2,1,0:T(8,128)(2,1)}) %all-gather.18.cloned.1.call-update) | async-done | bytes 2097168 | tf_op jit(solution)/shard_map/all_gather | solution.py:16
  118.6 6.0 while.29
  118.6 1.5 fusion.101
  120.1 1.5 fusion.101
  121.6 1.5 fusion.101
  123.2 1.5 fusion.101
  129.0 1.9 multiply_convert_fusion.4
  131.0 36.3 %all-gather.12.cloned.1.call-done = bf16[1024,2048]{0,1:T(8,128)(2,1)} async-done(((bf16[1024,64]{0,1:T(8,128)(2,1)}), bf16[1024,2048]{0,1:T(8,128)(2,1)}) %all-gather.12.cloned.1.call-update) | async-done | bytes 4194320 | tf_op jit(solution)/shard_map/all_gather | solution.py:230
  167.3 4.4 convolution_convert_fusion.5
  173.4 42.1 %all-reduce.9.cloned.1.call-done = bf16[256,2048]{1,0:T(8,128)(2,1)} async-done(((bf16[256,2048]{1,0:T(8,128)(2,1)}), bf16[256,2048]{1,0:T(8,128)(2,1)}) %all-reduce.9.cloned.1.call-update) | async-done | bytes 1048592 | tf_op jit(solution)/shard_map/psum | solution.py:106
  215.5 2.2 multiply_reduce_fusion
  218.8 55.0 %all-gather.14.cloned.1.call-done = bf16[2048,2048]{1,0:T(8,128)(2,1)} async-done(((bf16[64,2048]{1,0:T(8,128)(2,1)}), bf16[2048,2048]{1,0:T(8,128)(2,1)}) %all-gather.14.cloned.1.call-update) | async-done | bytes 8388624 | tf_op jit(solution)/shard_map/all_gather | solution.py:223
  273.8 7.1 fusion.71
  280.9 40.9 %all-gather.16.cloned.1.call-done = bf16[1024,2048]{0,1:T(8,128)(2,1)} async-done(((bf16[1024,64]{0,1:T(8,128)(2,1)}), bf16[1024,2048]{0,1:T(8,128)(2,1)}) %all-gather.16.cloned.1.call-update) | async-done | bytes 4194320 | tf_op jit(solution)/shard_map/all_gather | solution.py:230
  321.8 6.2 fusion.26
  329.1 3.3 convolution_convert_fusion.7
  332.5 43.6 %all-reduce.11.cloned.1.call-done = bf16[256,2048]{1,0:T(8,128)(2,1)} async-done(((bf16[256,2048]{1,0:T(8,128)(2,1)}), bf16[256,2048]{1,0:T(8,128)(2,1)}) %all-reduce.11.cloned.1.call-update) | async-done | bytes 1048592 | tf_op jit(solution)/shard_map/psum | solution.py:106
  376.1 2.6 fusion.7
  380.0 1.3 copy-done.73
  381.3 4.8 fusion.61
  386.1 2.5 copy.122
  388.6 1.8 multiply_reduce_fusion.2
  392.0 2.8 convolution_convert_fusion.9
  395.1 5.1 convolution_convert_fusion.2
  400.3 4.7 convolution_convert_fusion.4
  405.1 1.0 convolution_multiply_fusion
  406.2 1.4 convolution_bitcast_fusion.6
  407.6 1.8 fusion.16
  409.4 1.2 fusion.19
  410.7 2.1 convolution_bitcast_fusion.3
  412.8 15.3 %all-gather.20.cloned.1.call-done = bf16[8,256,512]{2,1,0:T(8,128)(2,1)} async-done(((bf16[2,256,512]{2,1,0:T(8,128)(2,1)}), bf16[8,256,512]{2,1,0:T(8,128)(2,1)}) %all-gather.20.cloned.1.call-update) | async-done | bytes 2097168 | tf_op jit(solution)/shard_map/all_gather | solution.py:37
  428.2 4.5 while.28
  428.2 1.4 convert_add_fusion.7
  429.6 1.4 convert_add_fusion.7
  431.0 1.4 convert_add_fusion.7
  432.7 3.1 fusion.15
  435.8 2.1 copy.121
  437.9 1.9 fusion.18
  441.0 9.4 %convolution_convert_fusion.6 = bf16[256,2048]{1,0:T(8,128)(2,1)} fusion(bf16[2048,3072]{1,0:T(8,128)(2,1)} %all-gather.10.cloned.1.call-done, bf16[256,1024]{1,0:T(8,128)(2,1)S(1)} %copy-done.37, bf16[256,1024]{1,0:T(8,128)(2,1)S(1)} %copy-done.20, bf16[256,512]{1,0:T(8,128)(2,1)S(1)} %bitcast.115, bf16[256,512]{1,0:T(8,128)(2,1)S(1)} %bitcast.117), kind=kOutput, calls=%fused_computation.17 | convolution fusion | flops 3228041216 | bytes 15204352 | tf_op jit(solution)/shard_map/dot_general | solution.py:90
  451.5 5.0 convolution_convert_fusion.3
  457.6 6.8 convolution_convert_fusion.1
  465.3 9.9 %convolution_convert_fusion = bf16[2048,3072]{1,0:T(8,128)(2,1)} fusion(bf16[256,1024]{1,0:T(8,128)(2,1)} %get-tuple-element.243, bf16[256,1024]{1,0:T(8,128)(2,1)S(1)} %copy-done.20, bf16[256,512]{1,0:T(8,128)(2,1)S(1)} %bitcast.116, bf16[256,512]{1,0:T(8,128)(2,1)S(1)} %bitcast.118, f32[256,2048]{1,0:T(8,128)} %param.18, f32[2048]{0:T(1024)S(1)} %copy-done.43, ...), kind=kOutput, calls=%fused_computation.5 | convolution fusion | flops 3235381248 | bytes 16262144 | tf_op jit(solution)/shard_map/dot_general | solution.py:96
  477.1 34.8 %reduce-scatter.11.cloned.1.call-done = bf16[1024,64]{0,1:T(8,128)(2,1)} async-done(((bf16[1024,2048]{0,1:T(8,128)(2,1)}), bf16[1024,64]{0,1:T(8,128)(2,1)}) %reduce-scatter.11.cloned.1.call-update) | async-done | bytes 131088 | tf_op jit(solution)/shard_map/reduce_scatter | solution.py:121
  511.9 1.6 convert_element_type.255
  513.5 61.5 %all-reduce.13.cloned.1.call-done = (bf16[256,2048]{1,0:T(8,128)(2,1)}, bf16[256,2048]{1,0:T(8,128)(2,1)}) async-done(((bf16[256,2048]{1,0:T(8,128)(2,1)}, bf16[256,2048]{1,0:T(8,128)(2,1)}), (bf16[256,2048]{1,0:T(8,128)(2,1)}, bf16[256,2048]{1,0:T(8,128)(2,1)})) %all-reduce.13.cloned.1.call-update) | async-done | bytes 2097168 | tf_op jit(solution)/shard_map/psum | solution.py:106
  575.1 2.7 fusion.8
  577.8 64.0 %all-reduce.3 = (bf16[2048]{0:T(1024)(128)(2,1)S(1)}, bf16[2048]{0:T(1024)(128)(2,1)S(1)}) all-reduce(bf16[2048]{0:T(1024)(128)(2,1)S(1)} %get-tuple-element.212, bf16[2048]{0:T(1024)(128)(2,1)S(1)} %copy-done.61), channel_id=5, replica_groups=mesh['dp'=8,'ctx'=4,'tp'=4] {'dp','ctx'}, use_global_device_ids=true, to_apply=%region_17.18.clone | all-reduce | flops 4096 | bytes 16384
  643.0 1.6 convert_add_fusion.2
  646.2 1.9 fusion.10
  648.1 10.7 %reduce-scatter.7.cloned.1.call-done = bf16[1024,64]{0,1:T(8,128)(2,1)} async-done(((bf16[1024,2048]{0,1:T(8,128)(2,1)}), bf16[1024,64]{0,1:T(8,128)(2,1)}) %reduce-scatter.7.cloned.1.call-update) | async-done | bytes 131088 | tf_op jit(solution)/shard_map/reduce_scatter | solution.py:121
  658.8 1.6 convert_element_type.251
  660.4 94.3 %reduce-scatter.9.cloned.1.call-done = bf16[64,2048]{1,0:T(8,128)(2,1)} async-done(((bf16[2048,2048]{1,0:T(8,128)(2,1)}), bf16[64,2048]{1,0:T(8,128)(2,1)}) %reduce-scatter.9.cloned.1.call-update) | async-done | bytes 262160 | tf_op jit(solution)/shard_map/reduce_scatter | solution.py:111
  754.7 1.8 fusion.78
  756.5 106.3 %reduce-scatter.5.cloned.1.call-done = bf16[64,3072]{1,0:T(8,128)(2,1)} async-done(((bf16[2048,3072]{1,0:T(8,128)(2,1)}), bf16[64,3072]{1,0:T(8,128)(2,1)}) %reduce-scatter.5.cloned.1.call-update) | async-done | bytes 393232 | tf_op jit(solution)/shard_map/reduce_scatter | solution.py:111
  862.8 1.6 fusion.77
  864.4 1.8 fusion.76
  (235 shorter events, 25.8 us)
Async XLA Ops:
  7.2 70.2 %copy-start = (f32[256,2048]{1,0:T(8,128)S(1)}, f32[256,2048]{1,0:T(8,128)}, u32[]{:S(2)}) copy-start(f32[256,2048]{1,0:T(8,128)} %param.18) | copy-start | bytes 6291460
  7.2 6.4 copy-start.71
  7.2 70.2 %copy-start.43 = (f32[2048]{0:T(1024)S(1)}, f32[2048]{0:T(1024)}, u32[]{:S(2)}) copy-start(f32[2048]{0:T(1024)} %param.20) | copy-start | bytes 24580
  7.2 70.1 %all-gather.10.cloned.1.call-start = ((), (), s32[]{:S(2)}) async-start(), calls=%async_computation.4 | async-start | bytes 12976128 | tf_op jit(solution)/shard_map/all_gather | solution.py:223
  9.2 109.4 %all-gather.18.cloned.1.call-start = ((), (), s32[]{:S(2)}) async-start(), calls=%async_computation.14 | async-start | bytes 2621440 | tf_op jit(solution)/shard_map/all_gather | solution.py:16
  14.3 69.6 %copy-start.68 = (f32[2]{0:T(128)}, f32[2]{0:T(128)S(1)}, u32[]{:S(2)}) copy-start(f32[2]{0:T(128)S(1)} %get-tuple-element.276) | copy-start | bytes 28
  14.3 69.6 %copy-start.53 = (f32[256]{0:T(256)}, f32[256]{0:T(256)S(1)}, u32[]{:S(2)}) copy-start(f32[256]{0:T(256)S(1)} %fusion.64) | copy-start | bytes 3076
  14.4 72.5 %copy-start.57 = (f32[256,2]{0,1:T(2,128)}, f32[256,2]{0,1:T(2,128)S(1)}, u32[]{:S(2)}) copy-start(f32[256,2]{0,1:T(2,128)S(1)} %get-tuple-element.275) | copy-start | bytes 6148
  14.4 110.8 %copy-start.48 = (f32[256,2]{0,1:T(2,128)}, f32[256,2]{0,1:T(2,128)S(1)}, u32[]{:S(2)}) copy-start(f32[256,2]{0,1:T(2,128)S(1)} %get-tuple-element.274) | copy-start | bytes 6148
  15.6 71.1 %copy-start.26 = (f32[256,128]{1,0:T(8,128)}, f32[256,128]{1,0:T(8,128)S(1)}, u32[]{:S(2)}) copy-start(f32[256,128]{1,0:T(8,128)S(1)} %get-tuple-element.273) | copy-start | bytes 393220
  85.5 40.8 %copy-start.10 = (bf16[256,1024]{1,0:T(8,128)(2,1)}, bf16[256,1024]{1,0:T(8,128)(2,1)S(1)}, u32[]{:S(2)}) copy-start(bf16[256,1024]{1,0:T(8,128)(2,1)S(1)} %slice.137) | copy-start | bytes 1572868
  86.6 2.5 copy-start.77
  86.7 12.3 %copy-start.65 = (s32[256]{0:T(256)S(1)}, s32[256]{0:T(256)}, u32[]{:S(2)}) copy-start(s32[256]{0:T(256)} %copy-done.64) | copy-start | bytes 3076
  86.7 12.4 %copy-start.69 = (f32[2]{0:T(128)S(1)}, f32[2]{0:T(128)}, u32[]{:S(2)}) copy-start(f32[2]{0:T(128)} %copy-done.68) | copy-start | bytes 28
  86.8 12.5 %copy-start.23 = (bf16[256,2,128]{2,0,1:T(8,128)(2,1)}, bf16[256,2,128]{2,0,1:T(8,128)(2,1)S(1)}, u32[]{:S(2)}) copy-start(bf16[256,2,128]{2,0,1:T(8,128)(2,1)S(1)} %get-tuple-element.270) | copy-start | bytes 393220
  88.4 78.9 %all-gather.12.cloned.1.call-start = ((), (), s32[]{:S(2)}) async-start(), calls=%async_computation.5 | async-start | bytes 4325376 | tf_op jit(solution)/shard_map/all_gather | solution.py:230
  89.1 126.3 %all-reduce.9.cloned.1.call-start = ((), (), s32[]{:S(2)}) async-start(), calls=%async_computation.6 | async-start | bytes 2097152 | tf_op jit(solution)/shard_map/psum | solution.py:106
  98.9 19.7 %copy-start.31 = (f32[256,256]{1,0:T(8,128)}, f32[256,256]{1,0:T(8,128)S(1)}, u32[]{:S(2)}) copy-start(f32[256,256]{1,0:T(8,128)S(1)} %maximum_convert_fusion) | copy-start | bytes 786436
  99.1 19.5 %copy-start.38 = (pred[256,256]{1,0:T(8,128)(4,1)}, pred[256,256]{1,0:T(8,128)(4,1)S(1)}, u32[]{:S(2)}) copy-start(pred[256,256]{1,0:T(8,128)(4,1)S(1)} %fusion.60) | copy-start | bytes 196612
  99.4 26.9 %copy-start.21 = (f32[2,256,256]{2,1,0:T(8,128)}, f32[2,256,256]{2,1,0:T(8,128)S(1)}, u32[]{:S(2)}) copy-start(f32[2,256,256]{2,1,0:T(8,128)S(1)} %convolution_multiply_fusion.1) | copy-start | bytes 1572868
  129.0 42.7 %copy-start.14 = (f32[256,1024]{1,0:T(8,128)}, f32[256,1024]{1,0:T(8,128)S(1)}, u32[]{:S(2)}) copy-start(f32[256,1024]{1,0:T(8,128)S(1)} %copy.120) | copy-start | bytes 3145732
  130.9 40.8 %copy-start.16 = (bf16[256,1024]{1,0:T(8,128)(2,1)}, bf16[256,1024]{1,0:T(8,128)(2,1)S(1)}, u32[]{:S(2)}) copy-start(bf16[256,1024]{1,0:T(8,128)(2,1)S(1)} %multiply_convert_fusion.4) | copy-start | bytes 1572868
  130.9 40.9 %copy-start.41 = (bf16[64,1024]{1,0:T(8,128)(2,1)S(1)}, bf16[64,1024]{1,0:T(8,128)(2,1)}, u32[]{:S(2)}) copy-start(bf16[64,1024]{1,0:T(8,128)(2,1)} %param.28) | copy-start | bytes 393220
  130.9 40.9 %copy-start.42 = (bf16[64,1024]{1,0:T(8,128)(2,1)S(1)}, bf16[64,1024]{1,0:T(8,128)(2,1)}, u32[]{:S(2)}) copy-start(bf16[64,1024]{1,0:T(8,128)(2,1)} %param.27) | copy-start | bytes 393220
  171.7 102.1 %all-gather.14.cloned.1.call-start = ((), (), s32[]{:S(2)}) async-start(), calls=%async_computation.7 | async-start | bytes 8650752 | tf_op jit(solution)/shard_map/all_gather | solution.py:223
  172.6 149.2 %all-gather.16.cloned.1.call-start = ((), (), s32[]{:S(2)}) async-start(), calls=%async_computation.8 | async-start | bytes 4325376 | tf_op jit(solution)/shard_map/all_gather | solution.py:230
  173.1 100.7 %copy-start.40 = (f32[2048]{0:T(1024)S(1)}, f32[2048]{0:T(1024)}, u32[]{:S(2)}) copy-start(f32[2048]{0:T(1024)} %param.21) | copy-start | bytes 24580
  173.1 202.9 %all-reduce.11.cloned.1.call-start = ((), (), s32[]{:S(2)}) async-start(), calls=%async_computation.9 | async-start | bytes 2097152 | tf_op jit(solution)/shard_map/psum | solution.py:106
  321.8 7.3 copy-start.72
  332.4 95.6 %all-gather.20.cloned.1.call-start = ((), (), s32[]{:S(2)}) async-start(), calls=%async_computation.15 | async-start | bytes 2621440 | tf_op jit(solution)/shard_map/all_gather | solution.py:37
  376.1 2.7 copy-start.67
  376.1 2.7 copy-start.9
  376.1 2.7 copy-start.13
  376.1 2.7 copy-start.51
  378.8 2.5 copy-start.73
  381.3 4.8 copy-start.6
  388.6 2.2 copy-start.8
  388.6 2.2 copy-start.47
  388.6 2.2 copy-start.60
  394.8 117.1 %reduce-scatter.11.cloned.1.call-start = ((), (), s32[]{:S(2)}) async-start(), calls=%async_computation.13 | async-start | bytes 4325376 | tf_op jit(solution)/shard_map/reduce_scatter | solution.py:121
  400.2 174.9 %all-reduce.13.cloned.1.call-start = ((), (), s32[]{:S(2)}) async-start(), calls=%async_computation.16 | async-start | bytes 4194304 | tf_op jit(solution)/shard_map/psum | solution.py:106
  400.3 4.8 copy-start.3
  400.3 4.8 copy-start.11
  400.3 4.8 copy-start.32
  400.3 4.8 copy-start.39
  400.3 4.8 copy-start.45
  400.3 4.8 copy-start.70
  405.1 2.5 copy-start.50
  406.2 3.3 copy-start.24
  407.6 3.1 copy-start.22
  410.7 17.5 %copy-start.75 = (bf16[4,2]{1,0:T(4,128)(2,1)S(1)}, bf16[4,2]{1,0:T(4,128)(2,1)}, u32[]{:S(2)}) copy-start(bf16[4,2]{1,0:T(4,128)(2,1)} %copy-done.74) | copy-start | bytes 52
  428.2 4.5 copy-start.25
  428.2 4.5 copy-start.58
  435.8 4.1 copy-start.27
  435.8 4.1 copy-start.33
  450.4 208.3 %reduce-scatter.7.cloned.1.call-start = ((), (), s32[]{:S(2)}) async-start(), calls=%async_computation.11 | async-start | bytes 4325376 | tf_op jit(solution)/shard_map/reduce_scatter | solution.py:121
  456.5 298.2 %reduce-scatter.9.cloned.1.call-start = ((), (), s32[]{:S(2)}) async-start(), calls=%async_computation.12 | async-start | bytes 8650752 | tf_op jit(solution)/shard_map/reduce_scatter | solution.py:111
  464.4 398.4 %reduce-scatter.5.cloned.1.call-start = ((), (), s32[]{:S(2)}) async-start(), calls=%async_computation.10 | async-start | bytes 12976128 | tf_op jit(solution)/shard_map/reduce_scatter | solution.py:111
  475.3 102.5 %copy-start.61 = (bf16[2048]{0:T(1024)(128)(2,1)S(1)}, bf16[2048]{0:T(1024)(128)(2,1)}, u32[]{:S(2)}) copy-start(bf16[2048]{0:T(1024)(128)(2,1)} %get-tuple-element.210) | copy-start | bytes 12292
  475.3 167.6 %copy-start.63 = (f32[256]{0:T(256)S(1)}, f32[256]{0:T(256)}, u32[]{:S(2)}) copy-start(f32[256]{0:T(256)} %copy-done.62) | copy-start | bytes 3076
  575.1 67.9 %copy-start.30 = (bf16[256,2048]{1,0:T(8,128)(2,1)S(1)}, bf16[256,2048]{1,0:T(8,128)(2,1)}, u32[]{:S(2)}) copy-start(bf16[256,2048]{1,0:T(8,128)(2,1)} %get-tuple-element.236) | copy-start | bytes 3145732
  642.9 2.4 copy-start.1
  643.0 3.0 copy-start.7
  643.0 3.2 copy-start.12
  (27 other events, 31.7 us)
Sparse Core Ops, SparseCore 0:
  10.9 66.3 all-gather.9
  88.5 30.0 all-gather.17
  120.9 46.3 all-gather.11
  171.9 43.5 all-reduce.8
  218.4 55.3 all-gather.13
  276.2 45.5 all-gather.15
  332.5 43.4 all-reduce.10
  394.9 33.0 all-gather.19
  431.7 80.1 reduce-scatter.10
  514.9 60.1 all-reduce.12
  578.7 80.0 reduce-scatter.6
  662.8 91.8 reduce-scatter.8
  758.5 104.1 reduce-scatter.4
where the time goes:
time: 882 us; the launch traced here: 873 us
  waiting for transfers between devices  623 us (71%)
  matrix products  92.3 us (10%)
  blocking collectives  72.1 us (8%)
  other arithmetic  38.4 us (4%)
  local copies, waits for them, and re-layouts  28.3 us (3%)
  between operations  17.4 us (2%)
    reduce_scatter x2, waiting for transfers between devices, send_rows(): lax.psum_scatter(members[0].astype(jnp.bfloat16), ('dp', 'ctx'), scatter_...  201 us
    psum x3, waiting for transfers between devices, heads_total(): return lax.psum(partial_sum.astype(jnp.bfloat16), 'tp').astype(jnp.float32)  147 us
    all_gather x2, waiting for transfers between devices, project_in(): lax.all_gather(weight, ('dp', 'ctx'), axis=0, tiled=True)  117 us
    all_gather x2, waiting for transfers between devices, project_out(): lax.all_gather(local_out[pick], ('dp', 'ctx'), axis=1, tiled=True)  77.2 us
    unnamed x2, blocking collectives  72.1 us
    reduce_scatter x2, waiting for transfers between devices, send_cols(): lax.psum_scatter(member.astype(jnp.bfloat16), ('dp', 'ctx'), scatter_dime...  45.4 us
    dot_general x4, matrix products, transposed_times(): lax.dot_general(left, right, (((0,), (0,)), ((), ())), preferred_element_...  26.9 us
    dot_general x4, matrix products, times_transposed(): lax.dot_general(left, right, (((1,), (1,)), ((), ())), preferred_element_...  23.7 us
  transfers between devices with their start and end apart: 13, of which 13 were waited for; matrix products, arithmetic and copies ran while one was open for 12% of the time, Pallas kernels for 0%

commit v1 on v0

v1 whole, which is shorter than its diff:
```python
import jax
import jax.numpy as jnp
import numpy as np
from jax import lax
from jax.sharding import Mesh, PartitionSpec as P

DK = 256
DV = 512
BF = jnp.bfloat16
F32 = jnp.float32
XY = ("x", "ctx")


def shift(value, axis, offset):
    n = lax.axis_size(axis)
    return lax.ppermute(value, axis, [(i, (i + offset) % n) for i in range(n)])


def shift_open(value, axis, offset):
    n = lax.axis_size(axis)
    return lax.ppermute(
        value, axis, [(i, i + offset) for i in range(n) if 0 <= i + offset < n]
    )


def swap(value):
    return lax.ppermute(value, "core", [(0, 1), (1, 0)])


def dot(left, right):
    return jnp.dot(left, right, preferred_element_type=F32)


def dot_t(left, right):
    return lax.dot_general(left, right, (((1,), (1,)), ((), ())), preferred_element_type=F32)


def t_dot(left, right):
    return lax.dot_general(left, right, (((0,), (0,)), ((), ())), preferred_element_type=F32)


def both(value):
    return jnp.concatenate((value, swap(value)), axis=0)


def heads_total(partial):
    rows = partial.shape[0] // 2
    low = partial[rows:].astype(BF)
    chip = partial[:rows] + swap(low).astype(F32)
    blocks = chip.astype(BF).reshape(4, rows // 4, -1)
    got = [shift(blocks[o], "tp", o) for o in (1, 2, 3)]
    mine = blocks[0].astype(F32)
    for part in got:
        mine = mine + part.astype(F32)
    mine = mine.astype(BF)
    parts = [mine] + [shift(mine, "tp", -o) for o in (1, 2, 3)]
    return jnp.concatenate(parts, axis=0).astype(F32)


def mean_scale(values, gain):
    factor = lax.rsqrt(jnp.mean(values * values, axis=-1, keepdims=True) + 1e-06)
    return values * factor * gain


def mean_scale_back(values, gain, grad):
    factor = lax.rsqrt(jnp.mean(values * values, axis=-1, keepdims=True) + 1e-06)
    unit = values * factor
    scaled = grad * gain
    out = factor * (scaled - unit * jnp.mean(scaled * unit, axis=-1, keepdims=True))
    part = jnp.sum((grad * unit).reshape(4, values.shape[0] // 4, -1), axis=1)
    return out, (part[0] + part[2]) + (part[1] + part[3])


def gate_norm(gate_pre, retained):
    centred = retained - jnp.mean(retained, axis=-1, keepdims=True)
    normed = centred * lax.rsqrt(jnp.mean(centred * centred, axis=-1, keepdims=True) + 1.0 * DK)
    return gate_pre * jax.nn.sigmoid(gate_pre) * normed


def gelu_gate(hidden, linear):
    return jax.nn.gelu(hidden, approximate=True) * linear


def rotate(values, cosine, sine):
    half = DK // 2
    first = values[:, :half]
    second = values[:, half:]
    return jnp.concatenate((first * cosine - second * sine, first * sine + second * cosine), axis=1)


def ein(spec, left, right):
    return jnp.einsum(spec, left, right, preferred_element_type=F32)


def columns_in(value):
    lead = value.shape[:-1]
    return value.reshape(*lead, 4, 2, 4, 64).swapaxes(-3, -2).reshape(*lead, 2048)


def columns_out(value):
    lead = value.shape[:-1]
    return value.reshape(*lead, 4, 4, 2, 64).swapaxes(-3, -2).reshape(*lead, 2048)


def roll_rows(value, amount):
    return lax.dynamic_slice_in_dim(jnp.concatenate((value, value), axis=0), amount, value.shape[0], 0)


def per_device(
    tokens,
    cotangent,
    gain_first,
    gain_second,
    w_query,
    w_key,
    w_value,
    w_gate,
    w_output,
    w_hidden,
    w_linear,
    w_down,
    decay_scale,
    first_length,
):
    rows = tokens.shape[0]
    core = lax.axis_index("core")
    place = lax.axis_index("ctx")
    plane = lax.axis_index("tp")

    def per_head(weight):
        return weight.reshape(weight.shape[0], 2, -1).swapaxes(0, 1)

    def gathered(weights):
        own = jnp.concatenate([per_head(w) for w in weights], axis=2)
        mine = lax.dynamic_index_in_dim(own, core, 0, False)
        theirs = swap(lax.dynamic_index_in_dim(own, 1 - core, 0, False))
        block = jnp.where(
            core == 0, jnp.concatenate((mine, theirs)), jnp.concatenate((theirs, mine))
        )
        return lax.all_gather(block, XY, axis=0, tiled=True)

    attn = gathered((w_query, w_key, w_value, w_gate))
    rest = gathered((w_output.T, w_hidden, w_linear, w_down.T))
    w_out_t = rest[:, :DV]
    w_mlp = rest[:, DV : 3 * DV]
    w_down_t = rest[:, 3 * DV :]

    tokens = columns_in(roll_rows(tokens, plane * (rows // 4)))
    cotangent = columns_in(roll_rows(cotangent, plane * (rows // 4)))
    gain_first = columns_in(gain_first)
    gain_second = columns_in(gain_second)

    rate = lax.dynamic_index_in_dim(decay_scale, core, 0, False) / 1024.0
    local = (jnp.arange(rows, dtype=jnp.int32) + plane * (rows // 4)) % rows
    index = place * rows + local
    lengths = jnp.concatenate((first_length, swap(first_length)))
    document = (index[None, :] >= lengths[:, None]).astype(jnp.int32)
    carried = (document == 0).astype(F32)
    steps = local.astype(F32)
    offsets = local[:, None] - local[None, :]
    linked = (offsets >= 0)[None] & (document[:, :, None] == document[:, None, :])
    mask = jnp.where(
        linked, jnp.exp(-rate * jnp.maximum(offsets, 0).astype(F32))[None], 0.0
    )
    enter = (carried * jnp.exp(-rate * (steps + 1.0))[None])[:, :, None]
    leave = jnp.exp(-rate * (rows - 1.0 - steps))[None, :, None]
    hop = jnp.exp(-rate * rows)
    half = DK // 2
    frequency = 10000.0 ** (-(jnp.arange(half).astype(F32) / half))
    angles = index.astype(F32)[:, None] * frequency[None, :]
    cosine = jnp.tile(jnp.cos(angles), (2, 1))
    sine = jnp.tile(jnp.sin(angles), (2, 1))

    def carry(state, way):
        low = state.astype(BF)
        near, mid, far = [shift_open(low, "ctx", way * o).astype(F32) for o in (1, 2, 3)]
        return near + hop * (mid + hop * far)

    normed_first = mean_scale(tokens, gain_first)
    x_first = both(normed_first.astype(BF))
    projected = dot(x_first, attn)
    query = rotate(projected[:, :DK], cosine, sine).astype(BF).reshape(2, rows, DK)
    key = rotate(projected[:, DK : 2 * DK], cosine, sine).astype(BF).reshape(2, rows, DK)
    value = projected[:, 2 * DK : 2 * DK + DV].astype(BF).reshape(2, rows, DV)
    gate_pre = projected[:, 2 * DK + DV :]
    key_out = (key.astype(F32) * leave).astype(BF)
    state_in = carry(ein("gjd,gje->gde", key_out, value), 1).astype(BF)
    weighted = (ein("gid,gjd->gij", query, key) * mask).astype(BF)
    inner = ein("gij,gje->gie", weighted, value)
    retained = (inner + ein("gid,gde->gie", query, state_in) * enter).reshape(2 * rows, DV)
    mixed_full, gate_back = jax.vjp(gate_norm, gate_pre, retained)
    mixed = mixed_full.astype(BF)
    hidden_state = tokens + heads_total(dot_t(mixed, w_out_t))
    normed_second = mean_scale(hidden_state, gain_second)
    x_second = both(normed_second.astype(BF))
    paired = dot(x_second, w_mlp)
    activated_full, gelu_back = jax.vjp(gelu_gate, paired[:, :DV], paired[:, DV:])
    activated = activated_full.astype(BF)
    layer_out = hidden_state + heads_total(dot_t(activated, w_down_t))
    g_out = both(cotangent.astype(BF))
    grad_hidden, grad_linear = gelu_back(dot(g_out, w_down_t))
    grad_pair = jnp.concatenate((grad_hidden, grad_linear), axis=1).astype(BF)
    grad_second = heads_total(dot_t(grad_pair, w_mlp))
    d_mlp = jnp.concatenate((t_dot(x_second, grad_pair), t_dot(g_out, activated)), axis=1).astype(BF)
    grad_state_part, gain_second_part = mean_scale_back(hidden_state, gain_second, grad_second)
    grad_state = cotangent + grad_state_part
    g_state = both(grad_state.astype(BF))
    grad_gate, grad_retained = gate_back(dot(g_state, w_out_t))
    grad_heads = grad_retained.reshape(2, rows, DV)
    grad_low = grad_heads.astype(BF)
    query_in = (query.astype(F32) * enter).astype(BF)
    state_back = carry(ein("gid,gie->gde", query_in, grad_low), -1).astype(BF)
    grad_scores = (ein("gie,gje->gij", grad_low, value) * mask).astype(BF)
    grad_query = ein("gij,gjd->gid", grad_scores, key) + enter * ein("gie,gde->gid", grad_low, state_in)
    grad_key = ein("gij,gid->gjd", grad_scores, query) + leave * ein("gje,gde->gjd", value, state_back)
    grad_value = ein("gij,gie->gje", weighted, grad_low) + ein("gjd,gde->gje", key_out, state_back)
    grad_proj = jnp.concatenate(
        (
            rotate(grad_query.reshape(2 * rows, DK), cosine, -sine),
            rotate(grad_key.reshape(2 * rows, DK), cosine, -sine),
            grad_value.reshape(2 * rows, DV),
            grad_gate,
        ),
        axis=1,
    ).astype(BF)
    d_attn = jnp.concatenate((t_dot(x_first, grad_proj), t_dot(g_state, mixed)), axis=1).astype(BF)
    grad_first = heads_total(dot_t(grad_proj, attn))
    grad_token_part, gain_first_part = mean_scale_back(tokens, gain_first, grad_first)
    input_grad = grad_state + grad_token_part

    def scattered(grad):
        block = lax.psum_scatter(grad, XY, scatter_dimension=0, tiled=True)
        block = block.reshape(2, 64, -1)
        mine = lax.dynamic_index_in_dim(block, core, 0, False)
        theirs = swap(lax.dynamic_index_in_dim(block, 1 - core, 0, False))
        return (
            jnp.where(core == 0, mine, theirs).astype(F32),
            jnp.where(core == 0, theirs, mine).astype(F32),
        )

    def wide(pair, start, stop):
        return jnp.concatenate((pair[0][:, start:stop], pair[1][:, start:stop]), axis=1)

    mlp_sum = scattered(d_mlp)
    attn_sum = scattered(d_attn)

    def gain_total(part):
        part = part + swap(part)
        for axis in XY:
            part = part + shift(part, axis, 1) + shift(part, axis, 2) + shift(part, axis, 3)
        spot = (lax.axis_index("x") * 4 + place) * 2 + core
        return lax.dynamic_slice_in_dim(part, spot * 64, 64, 0)

    gains = gain_total(jnp.stack((gain_first_part, gain_second_part)).T)

    def rows_out(value):
        return roll_rows(columns_out(value), rows - plane * (rows // 4))

    return (
        rows_out(layer_out),
        rows_out(input_grad),
        gains[:, 0],
        gains[:, 1],
        wide(attn_sum, 0, DK),
        wide(attn_sum, DK, 2 * DK),
        wide(attn_sum, 2 * DK, 2 * DK + DV),
        wide(attn_sum, 2 * DK + DV, 2 * DK + 2 * DV),
        wide(attn_sum, 2 * DK + 2 * DV, 2 * DK + 3 * DV).T,
        wide(mlp_sum, 0, DV),
        wide(mlp_sum, DV, 2 * DV),
        wide(mlp_sum, 2 * DV, 3 * DV).T,
    )


def solution(mesh):
    fine = Mesh(np.asarray(mesh.devices).reshape(4, 2, 4, 4), ("x", "core", "ctx", "tp"))
    split = ("x", "core", "ctx")
    row = P(split, None)
    win = P(split, "tp")
    wout = P("tp", split)
    in_specs = (row, row, P(), P(), win, win, win, win, wout, win, win, wout, P("tp"), P(("x", "core")))
    out_specs = (row, row, P(split), P(split), win, win, win, win, wout, win, win, wout)
    return jax.shard_map(
        per_device, mesh=fine, in_specs=in_specs, out_specs=out_specs, check_vma=False
    )
```

time: 882 us -> 527 us (0.60)
  waiting for transfers between devices: 623 us -> 180 us
  local copies, waits for them, and re-layouts: 28.3 us -> 140 us
  blocking collectives: 72.1 us -> 0 us
  starting transfers between devices: 1.21 us -> 68.2 us
  matrix products: 92.3 us -> 48.2 us
  other arithmetic: 38.4 us -> 64.4 us
    reduce_scatter x4 -> x2, waiting for transfers between devices: 246 us -> 0.02 us  [scattered(): block = lax.psum_scatter(grad, XY, scatter_dimension=0, tiled=True)]
    psum x3 -> x0, waiting for transfers between devices: 147 us -> none  [heads_total(): return lax.psum(partial_sum.astype(jnp.bfloat16), 'tp').astype(jnp.float32)]
    all_gather x6 -> x2, waiting for transfers between devices: 228 us -> 83 us  [gathered(): return lax.all_gather(block, XY, axis=0, tiled=True)]
    ppermute x0 -> x50, waiting for transfers between devices: none -> 96.5 us  [the longest x6 48.5 us: shift_open(): lax.ppermute(value, axis, [(i, i + offset) for i in range(n) if 0 <= i +...]
    unnamed x2 -> x0, blocking collectives: 72.1 us -> none
    ppermute x0 -> x50, starting transfers between devices: none -> 67.9 us  [the longest x30 38.8 us: shift(): return lax.ppermute(value, axis, [(i, (i + offset) % n) for i in range(n)])]
    concatenate x0 -> x33, local copies, waits for them, and re-layouts: none -> 67 us  [the longest x32 67 us: heads_total(): return jnp.concatenate(parts, axis=0).astype(F32)]
    dot_general x24, matrix products: 92.3 us -> 48.2 us  [the longest x4 15.7 us: dot(): return jnp.dot(left, right, preferred_element_type=F32)]
  transfers between devices with their start and end apart: 13 -> 54, of which waited for: 13 -> 24; matrix products, arithmetic and copies ran while one was open for 12% -> 42% of each run, Pallas kernels for 0% -> 0%
where the time goes in v1:
time: 527 us; the launch traced here: 517 us
  waiting for transfers between devices  180 us (34%)
  local copies, waits for them, and re-layouts  140 us (27%)
  starting transfers between devices  68.2 us (13%)
  other arithmetic  64.4 us (12%)
  matrix products  48.2 us (9%)
  between operations  17.2 us (3%)
    all_gather x2, waiting for transfers between devices, gathered(): return lax.all_gather(block, XY, axis=0, tiled=True)  83 us
    concatenate x32, local copies, waits for them, and re-layouts, heads_total(): return jnp.concatenate(parts, axis=0).astype(F32)  67 us
    ppermute x6, waiting for transfers between devices, shift_open(): lax.ppermute(value, axis, [(i, i + offset) for i in range(n) if 0 <= i +...  48.5 us
    ppermute x30, starting transfers between devices, shift(): return lax.ppermute(value, axis, [(i, (i + offset) % n) for i in range(n)])  38.8 us
    ppermute x30, waiting for transfers between devices, shift(): return lax.ppermute(value, axis, [(i, (i + offset) % n) for i in range(n)])  38.6 us
    unnamed x171, local copies, waits for them, and re-layouts  38.4 us
    dot_general x4, matrix products, dot(): return jnp.dot(left, right, preferred_element_type=F32)  15.7 us
    ppermute x14, starting transfers between devices, swap(): return lax.ppermute(value, 'core', [(0, 1), (1, 0)])  15.7 us
  transfers between devices with their start and end apart: 54, of which 24 were waited for; matrix products, arithmetic and copies ran while one was open for 42% of the time, Pallas kernels for 0%

profile of v1, /device:TPU:1, one launch (start us, length us, event | category | flops | bytes accessed | tf_op | source)
XLA Modules:
  0.0 517.2 jit_solution(16474322448527424029)
XLA Ops:
  22.2 3.0 multiply_reduce_fusion.4
  35.8 43.3 %all-gather.3.cloned.1.call-done = bf16[2048,1536]{1,0:T(8,128)(2,1)} async-done(((bf16[128,1536]{1,0:T(8,128)(2,1)}), bf16[2048,1536]{1,0:T(8,128)(2,1)}) %all-gather.3.cloned.1.call-update) | async-done | bytes 6291472 | tf_op jit(solution)/shard_map/all_gather | solution.py:140
  79.1 5.9 %fusion.22 = f32[512,1536]{1,0:T(8,128)S(1)} fusion(bf16[2048,1536]{1,0:T(8,128)(2,1)} %all-gather.3.cloned.1.call-done, bf16[256,2048]{0,1:T(8,128)(2,1)} %collective-permute-done, bf16[256,2048]{0,1:T(8,128)(2,1)S(1)} %multiply_convert_fusion.1), kind=kOutput, calls=%fused_computation.69 | convolution fusion | flops 3225419776 | bytes 11534336 | tf_op jit(solution)/shard_map/dot_general | solution.py:31
  86.2 3.1 collective-permute-start.3
  89.3 4.3 collective-permute-start.4
  96.2 10.7 %collective-permute-done.3 = bf16[2,256,512]{2,1,0:T(8,128)(2,1)S(1)} collective-permute-done((bf16[2,256,512]{2,1,0:T(8,128)(2,1)S(1)}, bf16[2,256,512]{2,1,0:T(8,128)(2,1)S(1)}, u32[]{:S(2)}, u32[]{:S(2)}) %collective-permute-start.3) | collective-permute-done | bytes 524320 | tf_op jit(solution)/shard_map/ppermute | solution.py:21
  106.9 12.7 %collective-permute-done.4 = bf16[2,256,512]{2,1,0:T(8,128)(2,1)S(1)} collective-permute-done((bf16[2,256,512]{2,1,0:T(8,128)(2,1)S(1)}, bf16[2,256,512]{2,1,0:T(8,128)(2,1)S(1)}, u32[]{:S(2)}, u32[]{:S(2)}) %collective-permute-start.4) | collective-permute-done | bytes 524320 | tf_op jit(solution)/shard_map/ppermute | solution.py:21
  119.5 3.8 collective-permute-done.5
  126.8 39.7 %all-gather.5.cloned.1.call-done = bf16[2048,2048]{1,0:T(8,128)(2,1)} async-done(((bf16[128,2048]{1,0:T(8,128)(2,1)}), bf16[2048,2048]{1,0:T(8,128)(2,1)}) %all-gather.5.cloned.1.call-update) | async-done | bytes 8388624 | tf_op jit(solution)/shard_map/all_gather | solution.py:140
  166.5 3.0 fusion.19
  170.4 2.3 collective-permute-done.7
  173.1 2.7 collective-permute-start.10
  177.5 9.1 %collective-permute-done.10 = bf16[64,2048]{1,0:T(8,128)(2,1)S(1)} collective-permute-done((bf16[64,2048]{1,0:T(8,128)(2,1)S(1)}, bf16[64,2048]{1,0:T(8,128)(2,1)S(1)}, u32[]{:S(2)}, u32[]{:S(2)}) %collective-permute-start.10) | collective-permute-done | bytes 262176 | tf_op jit(solution)/shard_map/ppermute | solution.py:16
  191.5 2.9 copy.119
  198.5 2.9 copy.125
  204.9 2.3 concatenate.178
  209.4 2.3 concatenate.179
  213.8 2.3 concatenate.180
  218.3 3.5 multiply_reduce_fusion.3
  223.4 2.3 collective-permute-start.14
  229.8 4.7 fusion.2
  243.0 2.4 convolution_convert_fusion.1
  245.4 3.4 pad_maximum_fusion.1
  248.8 8.6 %copy.154 = bf16[2048,1536]{1,0:T(8,128)(2,1)} copy(bf16[2048,1536]{0,1:T(8,128)(2,1)} %pad_maximum_fusion.1) | data formatting | bytes 12582912
  257.8 5.0 fusion
  266.2 2.5 collective-permute-start.17
  275.2 5.3 %collective-permute-done.17 = bf16[64,2048]{1,0:T(8,128)(2,1)S(1)} collective-permute-done((bf16[64,2048]{1,0:T(8,128)(2,1)S(1)}, bf16[64,2048]{1,0:T(8,128)(2,1)S(1)}, u32[]{:S(2)}, u32[]{:S(2)}) %collective-permute-start.17) | collective-permute-done | bytes 262176 | tf_op jit(solution)/shard_map/ppermute | solution.py:16
  281.4 3.3 collective-permute-start.19
  285.6 6.2 %collective-permute-done.25 = bf16[64,2048]{1,0:T(8,128)(2,1)S(1)} collective-permute-done((bf16[64,2048]{1,0:T(8,128)(2,1)S(1)}, bf16[64,2048]{1,0:T(8,128)(2,1)S(1)}, u32[]{:S(2)}, u32[]{:S(2)}) %collective-permute-start.25) | collective-permute-done | bytes 262176 | tf_op jit(solution)/shard_map/ppermute | solution.py:16
  292.6 2.6 collective-permute-start.27
  297.9 2.9 copy.134
  303.1 2.3 concatenate.193
  309.8 2.3 concatenate.185
  314.2 2.3 concatenate.186
  323.1 2.3 concatenate.194
  327.6 2.3 concatenate.195
  336.5 4.9 multiply_reduce_fusion.2
  343.6 6.2 %collective-permute-start.30 = (bf16[256,2048]{1,0:T(8,128)(2,1)S(1)}, bf16[256,2048]{1,0:T(8,128)(2,1)S(1)}, u32[]{:S(2)}, u32[]{:S(2)}) collective-permute-start(bf16[256,2048]{1,0:T(8,128)(2,1)S(1)} %add_convert_fusion), channel_id=1, source_target_pairs={{0,16},{16,0},{1,17},{17,1},{2,18},{18,2},{3,19},{19,3},{4,20},{20... | collective-permute-start | bytes 3145736 | tf_op jit(solution)/shard_map/ppermute | solution.py:27
  349.8 2.3 collective-permute-done.30
  352.1 3.1 multiply_reduce_fusion.5
  362.7 2.7 convolution_convert_fusion.3
  365.4 6.6 %collective-permute-done.31 = bf16[2,256,512]{2,1,0:T(8,128)(2,1)S(1)} collective-permute-done((bf16[2,256,512]{2,1,0:T(8,128)(2,1)S(1)}, bf16[2,256,512]{2,1,0:T(8,128)(2,1)S(1)}, u32[]{:S(2)}, u32[]{:S(2)}) %collective-permute-start.31) | collective-permute-done | bytes 524320 | tf_op jit(solution)/shard_map/ppermute | solution.py:21
  372.0 2.9 collective-permute-done.32
  374.9 11.9 %collective-permute-done.33 = bf16[2,256,512]{2,1,0:T(8,128)(2,1)S(1)} collective-permute-done((bf16[2,256,512]{2,1,0:T(8,128)(2,1)S(1)}, bf16[2,256,512]{2,1,0:T(8,128)(2,1)S(1)}, u32[]{:S(2)}, u32[]{:S(2)}) %collective-permute-start.33) | collective-permute-done | bytes 524320 | tf_op jit(solution)/shard_map/ppermute | solution.py:21
  389.4 6.6 %convolution_convert_fusion = bf16[2048,1536]{0,1:T(8,128)(2,1)} fusion(bf16[512,1536]{1,0:T(8,128)(2,1)S(1)} %constant_dynamic-update-slice_fusion, bf16[256,2048]{0,1:T(8,128)(2,1)} %collective-permute-done, bf16[256,2048]{0,1:T(8,128)(2,1)S(1)} %copy-done.34), kind=kOutput, calls=%fused_computation.1 | convolution fusion | flops 3228565504 | bytes 9961472 | tf_op jit(solution)/shard_map/dot_general | solution.py:39
  396.0 8.4 %pad_maximum_fusion = bf16[2048,2048]{0,1:T(8,128)(2,1)} fusion(bf16[2048,512]{0,1:T(8,128)(2,1)} %convolution_convert_fusion.3, bf16[2048,1536]{0,1:T(8,128)(2,1)} %convolution_convert_fusion), kind=kLoop, calls=%fused_computation | loop fusion | flops 16777216 | bytes 16777216 | tf_op jit(solution)/shard_map/concatenate | solution.py:226
  404.4 12.3 %copy.152 = bf16[2048,2048]{1,0:T(8,128)(2,1)} copy(bf16[2048,2048]{0,1:T(8,128)(2,1)} %pad_maximum_fusion) | data formatting | bytes 16777216
  416.7 6.0 %fusion.102 = f32[512,2048]{1,0:T(8,128)S(1)} fusion(bf16[512,1536]{1,0:T(8,128)(2,1)} %copy-done.62, bf16[2048,1536]{1,0:T(8,128)(2,1)} %all-gather.3.cloned.1.call-done), kind=kOutput, calls=%fused_computation.262 | convolution fusion | flops 3221225472 | bytes 12058624 | tf_op jit(solution)/shard_map/dot_general | solution.py:35
  423.5 2.3 collective-permute-done.34
  426.2 4.1 collective-permute-start.36
  430.3 5.3 %collective-permute-done.35 = bf16[64,2048]{1,0:T(8,128)(2,1)S(1)} collective-permute-done((bf16[64,2048]{1,0:T(8,128)(2,1)S(1)}, bf16[64,2048]{1,0:T(8,128)(2,1)S(1)}, u32[]{:S(2)}, u32[]{:S(2)}) %collective-permute-start.35) | collective-permute-done | bytes 262176 | tf_op jit(solution)/shard_map/ppermute | solution.py:16
  435.6 6.4 %collective-permute-done.36 = bf16[64,2048]{1,0:T(8,128)(2,1)S(1)} collective-permute-done((bf16[64,2048]{1,0:T(8,128)(2,1)S(1)}, bf16[64,2048]{1,0:T(8,128)(2,1)S(1)}, u32[]{:S(2)}, u32[]{:S(2)}) %collective-permute-start.36) | collective-permute-done | bytes 262176 | tf_op jit(solution)/shard_map/ppermute | solution.py:16
  442.1 2.8 collective-permute-start.38
  445.8 4.5 copy.142
  450.4 6.4 %reshape.646 = f32[4,64,2048]{2,1,0:T(8,128)} reshape(f32[256,4,4,2,64]{4,3,2,1,0:T(2,128)} %copy.142) | data formatting | bytes 4194304 | tf_op jit(solution)/shard_map/reshape | solution.py:97
  460.3 3.0 fusion.12
  466.7 2.3 concatenate.203
  471.2 2.3 concatenate.204
  475.7 2.4 multiply_reduce_fusion.1
  479.3 2.5 collective-permute-start.43
  483.0 3.8 multiply_add_fusion
  487.5 2.4 collective-permute-start.47
  489.9 3.5 fusion.4
  493.4 2.9 copy.145
  (387 shorter events, 149.0 us)
Async XLA Ops:
  7.2 72.0 %all-gather.3.cloned.1.call-start = ((), (), s32[]{:S(2)}) async-start(), calls=%async_computation.2 | async-start | bytes 6684672 | tf_op jit(solution)/shard_map/all_gather | solution.py:140
  12.2 2.6 collective-permute-start.1
  15.6 150.9 %all-gather.5.cloned.1.call-start = ((), (), s32[]{:S(2)}) async-start(), calls=%async_computation.3 | async-start | bytes 8912896 | tf_op jit(solution)/shard_map/all_gather | solution.py:140
  17.8 1.6 collective-permute-start.6
  20.3 477.9 %reduce-scatter.9.cloned.1.call-start = ((), (), s32[]{:S(2)}) async-start(), calls=%async_computation.5 | async-start | bytes 6684672 | tf_op jit(solution)/shard_map/reduce_scatter | solution.py:232
  26.9 58.1 %copy-start.52 = (f32[256]{0:T(256)}, f32[256]{0:T(256)S(1)}, u32[]{:S(2)}) copy-start(f32[256]{0:T(256)S(1)} %add_rsqrt_fusion.1) | copy-start | bytes 3076
  29.0 56.1 %copy-start.33 = (bf16[256,2048]{0,1:T(8,128)(2,1)}, bf16[256,2048]{0,1:T(8,128)(2,1)S(1)}, u32[]{:S(2)}) copy-start(bf16[256,2048]{0,1:T(8,128)(2,1)S(1)} %multiply_convert_fusion.1) | copy-start | bytes 3145732
  29.0 6.8 %collective-permute-start = (bf16[256,2048]{0,1:T(8,128)(2,1)S(1)}, bf16[256,2048]{0,1:T(8,128)(2,1)}, u32[]{:S(2)}, u32[]{:S(2)}) collective-permute-start(bf16[256,2048]{0,1:T(8,128)(2,1)S(1)} %multiply_convert_fusion.1), channel_id=1, source_target_pairs={{0,16},{16,0},{1,17},{17,1},{2,18},{18,2},{3,19},{19,3},{4,20},{20... | collective-permute-start | bytes 3145736 | tf_op jit(solution)/shard_map/ppermute | solution.py:27
  29.4 4.9 collective-permute-start.2
  30.9 54.2 %copy-start.63 = (s32[256]{0:T(256)}, s32[256]{0:T(256)S(1)}, u32[]{:S(2)}) copy-start(s32[256]{0:T(256)S(1)} %broadcast_add_fusion) | copy-start | bytes 3076
  33.5 51.8 %copy-start.27 = (f32[256,128]{1,0:T(8,128)}, f32[256,128]{1,0:T(8,128)S(1)}, u32[]{:S(2)}) copy-start(f32[256,128]{1,0:T(8,128)S(1)} %get-tuple-element.110) | copy-start | bytes 393220
  33.5 51.7 %copy-start.29 = (f32[256,128]{1,0:T(8,128)}, f32[256,128]{1,0:T(8,128)S(1)}, u32[]{:S(2)}) copy-start(f32[256,128]{1,0:T(8,128)S(1)} %get-tuple-element.111) | copy-start | bytes 393220
  35.1 50.0 %copy-start.68 = (s32[2]{0:T(128)}, s32[2]{0:T(128)S(1)}, u32[]{:S(2)}) copy-start(s32[2]{0:T(128)S(1)} %pad_add_fusion) | copy-start | bytes 28
  85.1 40.5 %copy-start.17 = (f32[512,1536]{1,0:T(8,128)}, f32[512,1536]{1,0:T(8,128)S(1)}, u32[]{:S(2)}) copy-start(f32[512,1536]{1,0:T(8,128)S(1)} %fusion.22) | copy-start | bytes 9437188
  85.4 38.1 %copy-start.22 = (bf16[512,128]{1,0:T(8,128)(2,1)}, bf16[512,128]{1,0:T(8,128)(2,1)S(1)}, u32[]{:S(2)}) copy-start(bf16[512,128]{1,0:T(8,128)(2,1)S(1)} %get-tuple-element.57) | copy-start | bytes 393220
  86.2 20.6 %collective-permute-start.3 = (bf16[2,256,512]{2,1,0:T(8,128)(2,1)S(1)}, bf16[2,256,512]{2,1,0:T(8,128)(2,1)S(1)}, u32[]{:S(2)}, u32[]{:S(2)}) collective-permute-start(bf16[2,256,512]{2,1,0:T(8,128)(2,1)S(1)} %convolution_convert_fusion.5), channel_id=1, source_target_pairs={{0,4},{4,8},{8,12},{1,5},{5,9},{9,13},{2,6},{6,10},{10,14},{3,7},{... | collective-permute-start | bytes 1572872 | tf_op jit(solution)/shard_map/ppermute | solution.py:21
  89.3 30.2 %collective-permute-start.4 = (bf16[2,256,512]{2,1,0:T(8,128)(2,1)S(1)}, bf16[2,256,512]{2,1,0:T(8,128)(2,1)S(1)}, u32[]{:S(2)}, u32[]{:S(2)}) collective-permute-start(bf16[2,256,512]{2,1,0:T(8,128)(2,1)S(1)} %convolution_convert_fusion.5), channel_id=1, source_target_pairs={{0,8},{4,12},{1,9},{5,13},{2,10},{6,14},{3,11},{7,15},{16,24},{20,... | collective-permute-start | bytes 1572872 | tf_op jit(solution)/shard_map/ppermute | solution.py:21
  93.7 29.6 %collective-permute-start.5 = (bf16[2,256,512]{2,1,0:T(8,128)(2,1)S(1)}, bf16[2,256,512]{2,1,0:T(8,128)(2,1)S(1)}, u32[]{:S(2)}, u32[]{:S(2)}) collective-permute-start(bf16[2,256,512]{2,1,0:T(8,128)(2,1)S(1)} %convolution_convert_fusion.5), channel_id=1, source_target_pairs={{0,12},{1,13},{2,14},{3,15},{16,28},{17,29},{18,30},{19,31},{32,44... | collective-permute-start | bytes 1572872 | tf_op jit(solution)/shard_map/ppermute | solution.py:21
  125.6 43.9 %copy-start.54 = (f32[512]{0:T(512)}, f32[512]{0:T(512)S(1)}, u32[]{:S(2)}) copy-start(f32[512]{0:T(512)S(1)} %rsqrt.37) | copy-start | bytes 6148
  125.6 43.9 %copy-start.56 = (f32[1,2,2,128]{3,1,2,0:T(2,128)}, f32[1,2,2,128]{3,1,2,0:T(2,128)S(1)}, u32[]{:S(2)}) copy-start(f32[1,2,2,128]{3,1,2,0:T(2,128)S(1)} %copy.160) | copy-start | bytes 6148
  169.7 3.0 collective-permute-start.7
  173.1 13.5 %collective-permute-start.10 = (bf16[64,2048]{1,0:T(8,128)(2,1)S(1)}, bf16[64,2048]{1,0:T(8,128)(2,1)S(1)}, u32[]{:S(2)}, u32[]{:S(2)}) collective-permute-start(bf16[64,2048]{1,0:T(8,128)(2,1)S(1)} %get-tuple-element.76), channel_id=1, source_target_pairs={{0,3},{1,0},{2,1},{3,2},{4,7},{5,4},{6,5},{7,6},{8,11},{9,8},{10,9... | collective-permute-start | bytes 786440 | tf_op jit(solution)/shard_map/ppermute | solution.py:16
  175.8 10.8 %collective-permute-start.8 = (bf16[64,2048]{1,0:T(8,128)(2,1)S(1)}, bf16[64,2048]{1,0:T(8,128)(2,1)S(1)}, u32[]{:S(2)}, u32[]{:S(2)}) collective-permute-start(bf16[64,2048]{1,0:T(8,128)(2,1)S(1)} %get-tuple-element.75), channel_id=1, source_target_pairs={{0,1},{1,2},{2,3},{3,0},{4,5},{5,6},{6,7},{7,4},{8,9},{9,10},{10,1... | collective-permute-start | bytes 786440 | tf_op jit(solution)/shard_map/ppermute | solution.py:16
  175.8 13.1 %collective-permute-start.9 = (bf16[64,2048]{1,0:T(8,128)(2,1)S(1)}, bf16[64,2048]{1,0:T(8,128)(2,1)S(1)}, u32[]{:S(2)}, u32[]{:S(2)}) collective-permute-start(bf16[64,2048]{1,0:T(8,128)(2,1)S(1)} %get-tuple-element.77), channel_id=1, source_target_pairs={{0,2},{1,3},{2,0},{3,1},{4,6},{5,7},{6,4},{7,5},{8,10},{9,11},{10,... | collective-permute-start | bytes 786440 | tf_op jit(solution)/shard_map/ppermute | solution.py:16
  189.0 15.9 %collective-permute-start.11 = (bf16[64,2048]{1,0:T(8,128)(2,1)S(1)}, bf16[64,2048]{1,0:T(8,128)(2,1)}, u32[]{:S(2)}, u32[]{:S(2)}) collective-permute-start(bf16[64,2048]{1,0:T(8,128)(2,1)S(1)} %add_convert_fusion.7), channel_id=1, source_target_pairs={{0,3},{1,0},{2,1},{3,2},{4,7},{5,4},{6,5},{7,6},{8,11},{9,8},{10,9... | collective-permute-start | bytes 786440 | tf_op jit(solution)/shard_map/ppermute | solution.py:16
  190.4 19.0 %collective-permute-start.12 = (bf16[64,2048]{1,0:T(8,128)(2,1)S(1)}, bf16[64,2048]{1,0:T(8,128)(2,1)}, u32[]{:S(2)}, u32[]{:S(2)}) collective-permute-start(bf16[64,2048]{1,0:T(8,128)(2,1)S(1)} %add_convert_fusion.7), channel_id=1, source_target_pairs={{0,2},{1,3},{2,0},{3,1},{4,6},{5,7},{6,4},{7,5},{8,10},{9,11},{10,... | collective-permute-start | bytes 786440 | tf_op jit(solution)/shard_map/ppermute | solution.py:16
  190.8 23.1 %collective-permute-start.13 = (bf16[64,2048]{1,0:T(8,128)(2,1)S(1)}, bf16[64,2048]{1,0:T(8,128)(2,1)}, u32[]{:S(2)}, u32[]{:S(2)}) collective-permute-start(bf16[64,2048]{1,0:T(8,128)(2,1)S(1)} %add_convert_fusion.7), channel_id=1, source_target_pairs={{0,1},{1,2},{2,3},{3,0},{4,5},{5,6},{6,7},{7,4},{8,9},{9,10},{10,1... | collective-permute-start | bytes 786440 | tf_op jit(solution)/shard_map/ppermute | solution.py:16
  223.4 6.4 %collective-permute-start.14 = (bf16[256,2048]{1,0:T(8,128)(2,1)S(1)}, bf16[256,2048]{1,0:T(8,128)(2,1)S(1)}, u32[]{:S(2)}, u32[]{:S(2)}) collective-permute-start(bf16[256,2048]{1,0:T(8,128)(2,1)S(1)} %multiply_convert_fusion), channel_id=1, source_target_pairs={{0,16},{16,0},{1,17},{17,1},{2,18},{18,2},{3,19},{19,3},{4,20},{20... | collective-permute-start | bytes 3145736 | tf_op jit(solution)/shard_map/ppermute | solution.py:27
  229.7 4.8 collective-permute-start.22
  241.0 22.1 %collective-permute-start.15 = (bf16[256,2048]{1,0:T(8,128)(2,1)}, bf16[256,2048]{1,0:T(8,128)(2,1)}, u32[]{:S(2)}, u32[]{:S(2)}) collective-permute-start(bf16[256,2048]{1,0:T(8,128)(2,1)} %slice.440), channel_id=1, source_target_pairs={{0,16},{16,0},{1,17},{17,1},{2,18},{18,2},{3,19},{19,3},{4,20},{20... | collective-permute-start | bytes 3145736 | tf_op jit(solution)/shard_map/ppermute | solution.py:27
  257.5 245.4 %reduce-scatter.7.cloned.1.call-start = ((), (), s32[]{:S(2)}) async-start(), calls=%async_computation.4 | async-start | bytes 8912896 | tf_op jit(solution)/shard_map/reduce_scatter | solution.py:232
  262.9 7.7 %collective-permute-start.23 = (bf16[256,2048]{1,0:T(8,128)(2,1)S(1)}, bf16[256,2048]{1,0:T(8,128)(2,1)S(1)}, u32[]{:S(2)}, u32[]{:S(2)}) collective-permute-start(bf16[256,2048]{1,0:T(8,128)(2,1)S(1)} %slice.439), channel_id=1, source_target_pairs={{0,16},{16,0},{1,17},{17,1},{2,18},{18,2},{3,19},{19,3},{4,20},{20... | collective-permute-start | bytes 3145736 | tf_op jit(solution)/shard_map/ppermute | solution.py:27
  264.7 8.7 %collective-permute-start.16 = (bf16[64,2048]{1,0:T(8,128)(2,1)S(1)}, bf16[64,2048]{1,0:T(8,128)(2,1)S(1)}, u32[]{:S(2)}, u32[]{:S(2)}) collective-permute-start(bf16[64,2048]{1,0:T(8,128)(2,1)S(1)} %get-tuple-element.72), channel_id=1, source_target_pairs={{0,1},{1,2},{2,3},{3,0},{4,5},{5,6},{6,7},{7,4},{8,9},{9,10},{10,1... | collective-permute-start | bytes 786440 | tf_op jit(solution)/shard_map/ppermute | solution.py:16
  266.2 14.3 %collective-permute-start.17 = (bf16[64,2048]{1,0:T(8,128)(2,1)S(1)}, bf16[64,2048]{1,0:T(8,128)(2,1)S(1)}, u32[]{:S(2)}, u32[]{:S(2)}) collective-permute-start(bf16[64,2048]{1,0:T(8,128)(2,1)S(1)} %get-tuple-element.74), channel_id=1, source_target_pairs={{0,2},{1,3},{2,0},{3,1},{4,6},{5,7},{6,4},{7,5},{8,10},{9,11},{10,... | collective-permute-start | bytes 786440 | tf_op jit(solution)/shard_map/ppermute | solution.py:16
  268.7 11.8 %collective-permute-start.18 = (bf16[64,2048]{1,0:T(8,128)(2,1)S(1)}, bf16[64,2048]{1,0:T(8,128)(2,1)S(1)}, u32[]{:S(2)}, u32[]{:S(2)}) collective-permute-start(bf16[64,2048]{1,0:T(8,128)(2,1)S(1)} %get-tuple-element.73), channel_id=1, source_target_pairs={{0,3},{1,0},{2,1},{3,2},{4,7},{5,4},{6,5},{7,6},{8,11},{9,8},{10,9... | collective-permute-start | bytes 786440 | tf_op jit(solution)/shard_map/ppermute | solution.py:16
  271.1 14.6 %collective-permute-start.24 = (bf16[64,2048]{1,0:T(8,128)(2,1)S(1)}, bf16[64,2048]{1,0:T(8,128)(2,1)S(1)}, u32[]{:S(2)}, u32[]{:S(2)}) collective-permute-start(bf16[64,2048]{1,0:T(8,128)(2,1)S(1)} %get-tuple-element.69), channel_id=1, source_target_pairs={{0,1},{1,2},{2,3},{3,0},{4,5},{5,6},{6,7},{7,4},{8,9},{9,10},{10,1... | collective-permute-start | bytes 786440 | tf_op jit(solution)/shard_map/ppermute | solution.py:16
  271.2 20.6 %collective-permute-start.25 = (bf16[64,2048]{1,0:T(8,128)(2,1)S(1)}, bf16[64,2048]{1,0:T(8,128)(2,1)S(1)}, u32[]{:S(2)}, u32[]{:S(2)}) collective-permute-start(bf16[64,2048]{1,0:T(8,128)(2,1)S(1)} %get-tuple-element.71), channel_id=1, source_target_pairs={{0,2},{1,3},{2,0},{3,1},{4,6},{5,7},{6,4},{7,5},{8,10},{9,11},{10,... | collective-permute-start | bytes 786440 | tf_op jit(solution)/shard_map/ppermute | solution.py:16
  273.4 18.4 %collective-permute-start.26 = (bf16[64,2048]{1,0:T(8,128)(2,1)S(1)}, bf16[64,2048]{1,0:T(8,128)(2,1)S(1)}, u32[]{:S(2)}, u32[]{:S(2)}) collective-permute-start(bf16[64,2048]{1,0:T(8,128)(2,1)S(1)} %get-tuple-element.70), channel_id=1, source_target_pairs={{0,3},{1,0},{2,1},{3,2},{4,7},{5,4},{6,5},{7,6},{8,11},{9,8},{10,9... | collective-permute-start | bytes 786440 | tf_op jit(solution)/shard_map/ppermute | solution.py:16
  281.4 15.5 %collective-permute-start.19 = (bf16[64,2048]{1,0:T(8,128)(2,1)}, bf16[64,2048]{1,0:T(8,128)(2,1)}, u32[]{:S(2)}, u32[]{:S(2)}) collective-permute-start(bf16[64,2048]{1,0:T(8,128)(2,1)} %add_convert_fusion.6), channel_id=1, source_target_pairs={{0,3},{1,0},{2,1},{3,2},{4,7},{5,4},{6,5},{7,6},{8,11},{9,8},{10,9... | collective-permute-start | bytes 786440 | tf_op jit(solution)/shard_map/ppermute | solution.py:16
  284.7 29.5 %collective-permute-start.20 = (bf16[64,2048]{1,0:T(8,128)(2,1)}, bf16[64,2048]{1,0:T(8,128)(2,1)}, u32[]{:S(2)}, u32[]{:S(2)}) collective-permute-start(bf16[64,2048]{1,0:T(8,128)(2,1)} %add_convert_fusion.6), channel_id=1, source_target_pairs={{0,2},{1,3},{2,0},{3,1},{4,6},{5,7},{6,4},{7,5},{8,10},{9,11},{10,... | collective-permute-start | bytes 786440 | tf_op jit(solution)/shard_map/ppermute | solution.py:16
  285.6 33.0 %collective-permute-start.21 = (bf16[64,2048]{1,0:T(8,128)(2,1)}, bf16[64,2048]{1,0:T(8,128)(2,1)}, u32[]{:S(2)}, u32[]{:S(2)}) collective-permute-start(bf16[64,2048]{1,0:T(8,128)(2,1)} %add_convert_fusion.6), channel_id=1, source_target_pairs={{0,1},{1,2},{2,3},{3,0},{4,5},{5,6},{6,7},{7,4},{8,9},{9,10},{10,1... | collective-permute-start | bytes 786440 | tf_op jit(solution)/shard_map/ppermute | solution.py:16
  292.6 30.5 %collective-permute-start.27 = (bf16[64,2048]{1,0:T(8,128)(2,1)}, bf16[64,2048]{1,0:T(8,128)(2,1)}, u32[]{:S(2)}, u32[]{:S(2)}) collective-permute-start(bf16[64,2048]{1,0:T(8,128)(2,1)} %add_convert_fusion.5), channel_id=1, source_target_pairs={{0,3},{1,0},{2,1},{3,2},{4,7},{5,4},{6,5},{7,6},{8,11},{9,8},{10,9... | collective-permute-start | bytes 786440 | tf_op jit(solution)/shard_map/ppermute | solution.py:16
  295.2 32.3 %collective-permute-start.28 = (bf16[64,2048]{1,0:T(8,128)(2,1)}, bf16[64,2048]{1,0:T(8,128)(2,1)}, u32[]{:S(2)}, u32[]{:S(2)}) collective-permute-start(bf16[64,2048]{1,0:T(8,128)(2,1)} %add_convert_fusion.5), channel_id=1, source_target_pairs={{0,2},{1,3},{2,0},{3,1},{4,6},{5,7},{6,4},{7,5},{8,10},{9,11},{10,... | collective-permute-start | bytes 786440 | tf_op jit(solution)/shard_map/ppermute | solution.py:16
  296.9 35.1 %collective-permute-start.29 = (bf16[64,2048]{1,0:T(8,128)(2,1)}, bf16[64,2048]{1,0:T(8,128)(2,1)}, u32[]{:S(2)}, u32[]{:S(2)}) collective-permute-start(bf16[64,2048]{1,0:T(8,128)(2,1)} %add_convert_fusion.5), channel_id=1, source_target_pairs={{0,1},{1,2},{2,3},{3,0},{4,5},{5,6},{6,7},{7,4},{8,9},{9,10},{10,1... | collective-permute-start | bytes 786440 | tf_op jit(solution)/shard_map/ppermute | solution.py:16
  343.6 8.4 %collective-permute-start.30 = (bf16[256,2048]{1,0:T(8,128)(2,1)S(1)}, bf16[256,2048]{1,0:T(8,128)(2,1)S(1)}, u32[]{:S(2)}, u32[]{:S(2)}) collective-permute-start(bf16[256,2048]{1,0:T(8,128)(2,1)S(1)} %add_convert_fusion), channel_id=1, source_target_pairs={{0,16},{16,0},{1,17},{17,1},{2,18},{18,2},{3,19},{19,3},{4,20},{20... | collective-permute-start | bytes 3145736 | tf_op jit(solution)/shard_map/ppermute | solution.py:27
  356.9 15.2 %collective-permute-start.31 = (bf16[2,256,512]{2,1,0:T(8,128)(2,1)S(1)}, bf16[2,256,512]{2,1,0:T(8,128)(2,1)S(1)}, u32[]{:S(2)}, u32[]{:S(2)}) collective-permute-start(bf16[2,256,512]{2,1,0:T(8,128)(2,1)S(1)} %convolution_convert_fusion.4), channel_id=1, source_target_pairs={{4,0},{8,4},{12,8},{5,1},{9,5},{13,9},{6,2},{10,6},{14,10},{7,3},{... | collective-permute-start | bytes 1572872 | tf_op jit(solution)/shard_map/ppermute | solution.py:21
  358.3 16.6 %collective-permute-start.32 = (bf16[2,256,512]{2,1,0:T(8,128)(2,1)S(1)}, bf16[2,256,512]{2,1,0:T(8,128)(2,1)S(1)}, u32[]{:S(2)}, u32[]{:S(2)}) collective-permute-start(bf16[2,256,512]{2,1,0:T(8,128)(2,1)S(1)} %convolution_convert_fusion.4), channel_id=1, source_target_pairs={{8,0},{12,4},{9,1},{13,5},{10,2},{14,6},{11,3},{15,7},{24,16},{28,... | collective-permute-start | bytes 1572872 | tf_op jit(solution)/shard_map/ppermute | solution.py:21
  359.6 27.2 %collective-permute-start.33 = (bf16[2,256,512]{2,1,0:T(8,128)(2,1)S(1)}, bf16[2,256,512]{2,1,0:T(8,128)(2,1)S(1)}, u32[]{:S(2)}, u32[]{:S(2)}) collective-permute-start(bf16[2,256,512]{2,1,0:T(8,128)(2,1)S(1)} %convolution_convert_fusion.4), channel_id=1, source_target_pairs={{12,0},{13,1},{14,2},{15,3},{28,16},{29,17},{30,18},{31,19},{44,32... | collective-permute-start | bytes 1572872 | tf_op jit(solution)/shard_map/ppermute | solution.py:21
  422.9 2.9 collective-permute-start.34
  426.1 9.4 %collective-permute-start.35 = (bf16[64,2048]{1,0:T(8,128)(2,1)S(1)}, bf16[64,2048]{1,0:T(8,128)(2,1)S(1)}, u32[]{:S(2)}, u32[]{:S(2)}) collective-permute-start(bf16[64,2048]{1,0:T(8,128)(2,1)S(1)} %get-tuple-element.66), channel_id=1, source_target_pairs={{0,1},{1,2},{2,3},{3,0},{4,5},{5,6},{6,7},{7,4},{8,9},{9,10},{10,1... | collective-permute-start | bytes 786440 | tf_op jit(solution)/shard_map/ppermute | solution.py:16
  426.2 15.8 %collective-permute-start.36 = (bf16[64,2048]{1,0:T(8,128)(2,1)S(1)}, bf16[64,2048]{1,0:T(8,128)(2,1)S(1)}, u32[]{:S(2)}, u32[]{:S(2)}) collective-permute-start(bf16[64,2048]{1,0:T(8,128)(2,1)S(1)} %get-tuple-element.68), channel_id=1, source_target_pairs={{0,2},{1,3},{2,0},{3,1},{4,6},{5,7},{6,4},{7,5},{8,10},{9,11},{10,... | collective-permute-start | bytes 786440 | tf_op jit(solution)/shard_map/ppermute | solution.py:16
  430.3 11.7 %collective-permute-start.37 = (bf16[64,2048]{1,0:T(8,128)(2,1)S(1)}, bf16[64,2048]{1,0:T(8,128)(2,1)S(1)}, u32[]{:S(2)}, u32[]{:S(2)}) collective-permute-start(bf16[64,2048]{1,0:T(8,128)(2,1)S(1)} %get-tuple-element.67), channel_id=1, source_target_pairs={{0,3},{1,0},{2,1},{3,2},{4,7},{5,4},{6,5},{7,6},{8,11},{9,8},{10,9... | collective-permute-start | bytes 786440 | tf_op jit(solution)/shard_map/ppermute | solution.py:16
  442.1 17.6 %collective-permute-start.38 = (bf16[64,2048]{1,0:T(8,128)(2,1)S(1)}, bf16[64,2048]{1,0:T(8,128)(2,1)S(1)}, u32[]{:S(2)}, u32[]{:S(2)}) collective-permute-start(bf16[64,2048]{1,0:T(8,128)(2,1)S(1)} %add_convert_fusion.4), channel_id=1, source_target_pairs={{0,3},{1,0},{2,1},{3,2},{4,7},{5,4},{6,5},{7,6},{8,11},{9,8},{10,9... | collective-permute-start | bytes 786440 | tf_op jit(solution)/shard_map/ppermute | solution.py:16
  444.9 14.8 %collective-permute-start.39 = (bf16[64,2048]{1,0:T(8,128)(2,1)S(1)}, bf16[64,2048]{1,0:T(8,128)(2,1)}, u32[]{:S(2)}, u32[]{:S(2)}) collective-permute-start(bf16[64,2048]{1,0:T(8,128)(2,1)S(1)} %add_convert_fusion.4), channel_id=1, source_target_pairs={{0,2},{1,3},{2,0},{3,1},{4,6},{5,7},{6,4},{7,5},{8,10},{9,11},{10,... | collective-permute-start | bytes 786440 | tf_op jit(solution)/shard_map/ppermute | solution.py:16
  445.1 15.3 %collective-permute-start.40 = (bf16[64,2048]{1,0:T(8,128)(2,1)S(1)}, bf16[64,2048]{1,0:T(8,128)(2,1)}, u32[]{:S(2)}, u32[]{:S(2)}) collective-permute-start(bf16[64,2048]{1,0:T(8,128)(2,1)S(1)} %add_convert_fusion.4), channel_id=1, source_target_pairs={{0,1},{1,2},{2,3},{3,0},{4,5},{5,6},{6,7},{7,4},{8,9},{9,10},{10,1... | collective-permute-start | bytes 786440 | tf_op jit(solution)/shard_map/ppermute | solution.py:16
  463.4 14.7 %collective-permute-start.41 = (f32[2048,2]{0,1:T(2,128)S(1)}, f32[2048,2]{0,1:T(2,128)S(1)}, u32[]{:S(2)}, u32[]{:S(2)}) collective-permute-start(f32[2048,2]{0,1:T(2,128)S(1)} %maximum_bitcast_fusion.2), channel_id=1, source_target_pairs={{0,16},{16,0},{1,17},{17,1},{2,18},{18,2},{3,19},{19,3},{4,20},{20... | collective-permute-start | bytes 49160 | tf_op jit(solution)/shard_map/ppermute | solution.py:27
  478.1 8.7 %collective-permute-start.42 = (f32[2048,2]{0,1:T(2,128)S(1)}, f32[2048,2]{0,1:T(2,128)S(1)}, u32[]{:S(2)}, u32[]{:S(2)}) collective-permute-start(f32[2048,2]{0,1:T(2,128)S(1)} %fusion.84), channel_id=1, source_target_pairs={{0,32},{32,64},{64,96},{96,0},{1,33},{33,65},{65,97},{97,1},{2,34}... | collective-permute-start | bytes 49160 | tf_op jit(solution)/shard_map/ppermute | solution.py:16
  479.3 7.5 %collective-permute-start.43 = (f32[2048,2]{0,1:T(2,128)S(1)}, f32[2048,2]{0,1:T(2,128)S(1)}, u32[]{:S(2)}, u32[]{:S(2)}) collective-permute-start(f32[2048,2]{0,1:T(2,128)S(1)} %fusion.84), channel_id=1, source_target_pairs={{0,64},{32,96},{64,0},{96,32},{1,65},{33,97},{65,1},{97,33},{2,66}... | collective-permute-start | bytes 49160 | tf_op jit(solution)/shard_map/ppermute | solution.py:16
  481.8 5.1 collective-permute-start.44
  486.9 11.2 %collective-permute-start.45 = (f32[2048,2]{0,1:T(2,128)S(1)}, f32[2048,2]{0,1:T(2,128)S(1)}, u32[]{:S(2)}, u32[]{:S(2)}) collective-permute-start(f32[2048,2]{0,1:T(2,128)S(1)} %add_add_fusion.1), channel_id=1, source_target_pairs={{0,4},{4,8},{8,12},{12,0},{1,5},{5,9},{9,13},{13,1},{2,6},{6,10},{... | collective-permute-start | bytes 49160 | tf_op jit(solution)/shard_map/ppermute | solution.py:16
  487.0 11.1 %collective-permute-start.46 = (f32[2048,2]{0,1:T(2,128)S(1)}, f32[2048,2]{0,1:T(2,128)S(1)}, u32[]{:S(2)}, u32[]{:S(2)}) collective-permute-start(f32[2048,2]{0,1:T(2,128)S(1)} %add_add_fusion.1), channel_id=1, source_target_pairs={{0,8},{4,12},{8,0},{12,4},{1,9},{5,13},{9,1},{13,5},{2,10},{6,14},... | collective-permute-start | bytes 49160 | tf_op jit(solution)/shard_map/ppermute | solution.py:16
  487.5 10.6 %collective-permute-start.47 = (f32[2048,2]{0,1:T(2,128)S(1)}, f32[2048,2]{0,1:T(2,128)S(1)}, u32[]{:S(2)}, u32[]{:S(2)}) collective-permute-start(f32[2048,2]{0,1:T(2,128)S(1)} %add_add_fusion.1), channel_id=1, source_target_pairs={{0,12},{4,0},{8,4},{12,8},{1,13},{5,1},{9,5},{13,9},{2,14},{6,2},{... | collective-permute-start | bytes 49160 | tf_op jit(solution)/shard_map/ppermute | solution.py:16
  499.2 2.6 collective-permute-start.49
  503.9 2.6 collective-permute-start.48
  (67 other events, 498.2 us)
Sparse Core Ops, SparseCore 0:
  15.7 63.3 all-gather.2
  81.9 84.5 all-gather.4
  257.6 80.2 reduce-scatter.8
  416.9 83.4 reduce-scatter.6

commit v2 on v1

v2 whole, which is shorter than its diff:
```python
import jax
import jax.numpy as jnp
import numpy as np
from jax import lax
from jax.experimental import pallas as pl
from jax.experimental.pallas import tpu as pltpu
from jax.sharding import Mesh, PartitionSpec as P

D = 2048
DK = 256
DV = 512
SLAB = 512
BF = jnp.bfloat16
F32 = jnp.float32
XY = ("x", "ctx")
MIB = 1 << 20


def shift(value, axis, offset):
    n = lax.axis_size(axis)
    return lax.ppermute(value, axis, [(i, (i + offset) % n) for i in range(n)])


def shift_open(value, axis, offset):
    n = lax.axis_size(axis)
    return lax.ppermute(
        value, axis, [(i, i + offset) for i in range(n) if 0 <= i + offset < n]
    )


def swap(value):
    return lax.ppermute(value, "core", [(0, 1), (1, 0)])


def after(value, *earlier):
    return lax.optimization_barrier((value, *earlier))[0]


def call(body, grid, ins, outs, shapes, scalars, operands, name, flops=0, scratch=()):
    nbytes = sum(a.size * a.dtype.itemsize for a in jax.tree.leaves((operands, shapes)))
    return pl.pallas_call(
        body,
        out_shape=shapes,
        grid_spec=pltpu.PrefetchScalarGridSpec(
            num_scalar_prefetch=1, grid=grid, in_specs=ins, out_specs=outs, scratch_shapes=scratch
        ),
        compiler_params=pltpu.CompilerParams(
            vmem_limit_bytes=48 * MIB, dimension_semantics=("arbitrary",) * len(grid)
        ),
        cost_estimate=pl.CostEstimate(flops=flops, bytes_accessed=nbytes, transcendentals=0),
        name=name,
    )(scalars, *operands)


def whole(array):
    return pl.BlockSpec(array.shape, lambda *_: (0,) * array.ndim)


def sds(shape, dtype):
    return jax.ShapeDtypeStruct(shape, dtype)


def slab_rows(ref, core):
    return jnp.concatenate(
        [ref[0, y, jnp.bitwise_xor(c, core)] for c in (0, 1) for y in range(4)], axis=0
    )


def mm_in(left, right, weight, start, width, scalars, name):
    def body(s_ref, a_ref, b_ref, w_ref, out_ref):
        step = pl.program_id(0)
        part = jnp.dot(
            jnp.concatenate((a_ref[...], b_ref[...]), axis=0),
            slab_rows(w_ref, s_ref[0]),
            preferred_element_type=F32,
        )

        @pl.when(step == 0)
        def _():
            out_ref[...] = part

        @pl.when(step > 0)
        def _():
            out_ref[...] += part

    rows = left.shape[0]
    cols = pl.BlockSpec((rows, SLAB), lambda i, s: (0, i))
    return call(
        body,
        (4,),
        [cols, cols, pl.BlockSpec((1, 4, 2, 64, width), lambda i, s: (i, 0, 0, 0, start // width))],
        pl.BlockSpec((2 * rows, width), lambda i, s: (0, 0)),
        sds((2 * rows, width), F32),
        scalars,
        (left, right, weight),
        name,
        flops=4 * rows * D * width,
    )


def mm_back(grad, weight, start, scalars, name):
    rows, width = grad.shape
    half = rows // 2

    def body(s_ref, g_ref, w_ref, own_ref, other_ref):
        out = lax.dot_general(
            g_ref[...],
            slab_rows(w_ref, s_ref[0]),
            (((1,), (1,)), ((), ())),
            preferred_element_type=F32,
        )
        own_ref[...] = out[:half]
        other_ref[...] = out[half:].astype(BF)

    cols = pl.BlockSpec((half, SLAB), lambda i, s: (0, i))
    return call(
        body,
        (4,),
        [whole(grad), pl.BlockSpec((1, 4, 2, 64, width), lambda i, s: (i, 0, 0, 0, start // width))],
        (cols, cols),
        (sds((half, D), F32), sds((half, D), BF)),
        scalars,
        (grad, weight),
        name,
        flops=2 * rows * D * width,
    )


def mm_weight(pairs, scalars, name):
    widths = [grad.shape[1] for _, grad in pairs]
    rows = pairs[0][0][0].shape[0]

    def body(s_ref, *refs):
        out_ref = refs[-1]
        at = 0
        for k, width in enumerate(widths):
            a_ref, b_ref, g_ref = refs[3 * k : 3 * k + 3]
            out = lax.dot_general(
                jnp.concatenate((a_ref[...], b_ref[...]), axis=0),
                g_ref[...],
                (((0,), (0,)), ((), ())),
                preferred_element_type=F32,
            ).astype(BF)
            for c in (0, 1):
                for y in range(4):
                    first = (c * 4 + y) * 64
                    out_ref[0, y, jnp.bitwise_xor(c, s_ref[0]), :, at : at + width] = out[
                        first : first + 64
                    ]
            at += width

    cols = pl.BlockSpec((rows, SLAB), lambda i, s: (0, i))
    specs, operands = [], []
    for (a, b), grad in pairs:
        specs += [cols, cols, whole(grad)]
        operands += [a, b, grad]
    total = sum(widths)
    return call(
        body,
        (4,),
        specs,
        pl.BlockSpec((1, 4, 2, 64, total), lambda i, s: (i, 0, 0, 0, 0)),
        sds((4, 4, 2, 64, total), BF),
        scalars,
        tuple(operands),
        name,
        flops=4 * rows * D * total,
    )


def split_heads(weights, turned, scalars, name):
    widths = [(w.shape[0] if t else w.shape[1]) // 2 for w, t in zip(weights, turned)]

    def body(s_ref, *refs):
        mine_ref, theirs_ref = refs[-2:]
        core = s_ref[0]
        for out_ref, head in ((mine_ref, core), (theirs_ref, 1 - core)):
            at = 0
            for ref, width, turn in zip(refs, widths, turned):
                if turn:
                    piece = ref[pl.ds(pl.multiple_of(head * width, width), width), :]
                    piece = piece.astype(F32).T.astype(BF)
                else:
                    piece = ref[:, pl.ds(pl.multiple_of(head * width, width), width)]
                out_ref[:, at : at + width] = piece
                at += width

    total = sum(widths)
    spec = pl.BlockSpec((64, total), lambda i, s: (0, 0))
    return call(
        body,
        (1,),
        [whole(w) for w in weights],
        (spec, spec),
        (sds((64, total), BF),) * 2,
        scalars,
        tuple(weights),
        name,
    )


def join_heads(mine, theirs, widths, turned, scalars, name):
    def body(s_ref, mine_ref, theirs_ref, *outs):
        core = s_ref[0]
        for in_ref, head in ((mine_ref, core), (theirs_ref, 1 - core)):
            at = 0
            for ref, width, turn in zip(outs, widths, turned):
                piece = in_ref[:, at : at + width].astype(F32)
                span = pl.ds(pl.multiple_of(head * width, width), width)
                if turn:
                    ref[span, :] = piece.T
                else:
                    ref[:, span] = piece
                at += width

    shapes = tuple(
        sds((2 * w, 64) if t else (64, 2 * w), F32) for w, t in zip(widths, turned)
    )
    return call(
        body,
        (1,),
        [whole(mine), whole(theirs)],
        tuple(whole(s) for s in shapes),
        shapes,
        scalars,
        (mine, theirs),
        name,
    )


def scale_of(values):
    return lax.rsqrt(jnp.mean(values * values, axis=-1, keepdims=True) + 1e-06)


def turned_spec(rows):
    return pl.BlockSpec((rows, D), lambda i, s: (lax.rem(i + s[1], 4), 0))


def plain_spec(rows):
    return pl.BlockSpec((rows, D), lambda i, s: (i, 0))


def enter_rows(tokens, cotangent, gain, scalars):
    rows = tokens.shape[0]
    block = rows // 4

    def body(s_ref, t_ref, c_ref, g_ref, t_out, c_out, n_out, l_out):
        values = t_ref[...]
        t_out[...] = values
        n_out[...] = (values * scale_of(values) * g_ref[...]).astype(BF)
        c_out[...] = c_ref[...]
        l_out[...] = c_ref[...].astype(BF)

    turn, plain = turned_spec(block), plain_spec(block)
    full = (rows, D)
    return call(
        body,
        (4,),
        [turn, turn, whole(gain)],
        (plain,) * 4,
        (sds(full, F32), sds(full, F32), sds(full, BF), sds(full, BF)),
        scalars,
        (tokens, cotangent, gain),
        "enter_rows",
    )


def each_part(refs, work):
    step = pl.program_id(0)
    for k, ref in enumerate(refs):

        @pl.when(step == k)
        def _(ref=ref):
            work(ref[...].astype(F32))


def second_norm(tokens, parts, gain, scalars):
    rows = tokens.shape[0]
    block = rows // 4

    def body(s_ref, t_ref, g_ref, *refs):
        h_out, n_out = refs[4:]

        def work(part):
            values = t_ref[...] + part
            h_out[...] = values
            n_out[...] = (values * scale_of(values) * g_ref[...]).astype(BF)

        each_part(refs[:4], work)

    plain = plain_spec(block)
    return call(
        body,
        (4,),
        [plain, whole(gain)] + [whole(p) for p in parts],
        (plain, plain),
        (sds((rows, D), F32), sds((rows, D), BF)),
        scalars,
        (tokens, gain, *parts),
        "second_norm",
    )


def leave_rows(hidden, parts, scalars):
    rows = hidden.shape[0]
    block = rows // 4

    def body(s_ref, h_ref, *refs):
        def work(part):
            refs[4][...] = h_ref[...] + part

        each_part(refs[:4], work)

    return call(
        body,
        (4,),
        [plain_spec(block)] + [whole(p) for p in parts],
        turned_spec(block),
        sds((rows, D), F32),
        scalars,
        (hidden, *parts),
        "leave_rows",
    )


def norm_back(values, upstream, parts, gain, last, scalars, name):
    rows = values.shape[0]
    block = rows // 4

    def body(s_ref, v_ref, u_ref, g_ref, *refs):
        outs = refs[4:]

        def work(part):
            values = v_ref[...]
            factor = scale_of(values)
            unit = values * factor
            scaled = part * g_ref[...]
            out = u_ref[...] + factor * (
                scaled - unit * jnp.mean(scaled * unit, axis=-1, keepdims=True)
            )
            outs[0][...] = out
            outs[1][0] = jnp.sum(part * unit, axis=0, keepdims=True)
            if not last:
                outs[2][...] = out.astype(BF)

        each_part(refs[:4], work)

    plain = plain_spec(block)
    specs = [turned_spec(block) if last else plain, pl.BlockSpec((1, 1, D), lambda i, s: (i, 0, 0))]
    shapes = [sds((rows, D), F32), sds((4, 1, D), F32)]
    if not last:
        specs.append(plain)
        shapes.append(sds((rows, D), BF))
    out = call(
        body,
        (4,),
        [plain, plain, whole(gain)] + [whole(p) for p in parts],
        tuple(specs),
        tuple(shapes),
        scalars,
        (values, upstream, gain, *parts),
        name,
    )
    gains = out[1][:, 0]
    return (out[0], (gains[0] + gains[2]) + (gains[1] + gains[3]), *out[2:])


def heads_total(own, other):
    came = swap(other)
    block = own.shape[0] // 4
    blocks = [
        (own[o * block : (o + 1) * block] + came[o * block : (o + 1) * block].astype(F32)).astype(BF)
        for o in range(4)
    ]
    got = [shift(blocks[o], "tp", o) for o in (1, 3, 2)]
    mine = blocks[0].astype(F32)
    for part in got:
        mine = mine + part.astype(F32)
    mine = mine.astype(BF)
    near, far, mid = [shift(mine, "tp", -o) for o in (1, 3, 2)]
    return (mine, near, mid, far)


def gate_norm(gate_pre, retained):
    centred = retained - jnp.mean(retained, axis=-1, keepdims=True)
    normed = centred * lax.rsqrt(jnp.mean(centred * centred, axis=-1, keepdims=True) + 1.0 * DK)
    return gate_pre * jax.nn.sigmoid(gate_pre) * normed


def gelu_gate(hidden, linear):
    return jax.nn.gelu(hidden, approximate=True) * linear


def rotate(values, cosine, sine):
    half = DK // 2
    first = values[:, :half]
    second = values[:, half:]
    return jnp.concatenate((first * cosine - second * sine, first * sine + second * cosine), axis=1)


def ein(spec, left, right):
    return jnp.einsum(spec, left, right, preferred_element_type=F32)


def per_device(
    tokens,
    cotangent,
    gain_first,
    gain_second,
    w_query,
    w_key,
    w_value,
    w_gate,
    w_output,
    w_hidden,
    w_linear,
    w_down,
    decay_scale,
    first_length,
):
    rows = tokens.shape[0]
    core = lax.axis_index("core")
    place = lax.axis_index("ctx")
    plane = lax.axis_index("tp")
    scalars = jnp.stack((core, plane)).astype(jnp.int32)

    def gathered(mine, theirs):
        block = jnp.concatenate((mine, swap(theirs)), axis=0)
        return lax.all_gather(block, XY, axis=0, tiled=True).reshape(4, 4, 2, 64, -1)

    attn_split = split_heads(
        (w_query, w_key, w_value, w_gate), (False,) * 4, scalars, "split_attn"
    )
    attn = gathered(*attn_split)
    rest = gathered(
        *split_heads(
            after((w_hidden, w_linear, w_output, w_down), attn_split[0]),
            (False, False, True, True),
            scalars,
            "split_rest",
        )
    )
    tokens, cotangent = after((tokens, cotangent), attn_split[0])
    gain_first = gain_first.reshape(1, D)
    gain_second = gain_second.reshape(1, D)
    tokens, cotangent, normed_first, cot_low = enter_rows(tokens, cotangent, gain_first, scalars)

    rate = lax.dynamic_index_in_dim(decay_scale, core, 0, False) / 1024.0
    local = (jnp.arange(rows, dtype=jnp.int32) + plane * (rows // 4)) % rows
    index = place * rows + local
    lengths = jnp.concatenate((first_length, swap(first_length)))
    document = (index[None, :] >= lengths[:, None]).astype(jnp.int32)
    carried = (document == 0).astype(F32)
    steps = local.astype(F32)
    offsets = local[:, None] - local[None, :]
    linked = (offsets >= 0)[None] & (document[:, :, None] == document[:, None, :])
    mask = jnp.where(
        linked, jnp.exp(-rate * jnp.maximum(offsets, 0).astype(F32))[None], 0.0
    )
    enter = (carried * jnp.exp(-rate * (steps + 1.0))[None])[:, :, None]
    leave = jnp.exp(-rate * (rows - 1.0 - steps))[None, :, None]
    hop = jnp.exp(-rate * rows)
    half = DK // 2
    frequency = 10000.0 ** (-(jnp.arange(half).astype(F32) / half))
    angles = index.astype(F32)[:, None] * frequency[None, :]
    cosine = jnp.tile(jnp.cos(angles), (2, 1))
    sine = jnp.tile(jnp.sin(angles), (2, 1))

    def carry(state, way):
        low = state.astype(BF)
        near, mid, far = [shift_open(low, "ctx", way * o).astype(F32) for o in (1, 2, 3)]
        return near + hop * (mid + hop * far)

    x_first = (normed_first, swap(normed_first))
    projected = mm_in(*x_first, attn, 0, 1536, scalars, "project_attn")
    query = rotate(projected[:, :DK], cosine, sine).astype(BF).reshape(2, rows, DK)
    key = rotate(projected[:, DK : 2 * DK], cosine, sine).astype(BF).reshape(2, rows, DK)
    value = projected[:, 2 * DK : 2 * DK + DV].astype(BF).reshape(2, rows, DV)
    gate_pre = projected[:, 2 * DK + DV :]
    key_out = (key.astype(F32) * leave).astype(BF)
    state_in = carry(ein("gjd,gje->gde", key_out, value), 1).astype(BF)
    weighted = (ein("gid,gjd->gij", query, key) * mask).astype(BF)
    inner = ein("gij,gje->gie", weighted, value)
    retained = (inner + ein("gid,gde->gie", query, state_in) * enter).reshape(2 * rows, DV)
    mixed_full, gate_back = jax.vjp(gate_norm, gate_pre, retained)
    mixed = mixed_full.astype(BF)
    parts = heads_total(*mm_back(mixed, rest, 2 * DV, scalars, "project_out"))
    g_out = (cot_low, swap(cot_low))
    grad_activated = mm_in(*g_out, rest, 3 * DV, DV, scalars, "back_down")
    hidden_state, normed_second = second_norm(tokens, parts, gain_second, scalars)
    x_second = (normed_second, swap(normed_second))
    paired = mm_in(*x_second, rest, 0, 2 * DV, scalars, "project_mlp")
    activated_full, gelu_back = jax.vjp(gelu_gate, paired[:, :DV], paired[:, DV:])
    activated = activated_full.astype(BF)
    grad_pair = jnp.concatenate(gelu_back(grad_activated), axis=1).astype(BF)
    parts = heads_total(*mm_back(grad_pair, rest, 0, scalars, "back_mlp"))
    layer_parts = heads_total(*mm_back(activated, rest, 3 * DV, scalars, "project_down"))
    layer_out = leave_rows(hidden_state, layer_parts, scalars)
    d_mlp = mm_weight(
        ((x_second, grad_pair), (g_out, activated)), scalars, "weight_mlp"
    )
    grad_state, gain_second_part, grad_state_low = norm_back(
        hidden_state, cotangent, parts, gain_second, False, scalars, "second_back"
    )
    g_state = (grad_state_low, swap(grad_state_low))
    grad_mixed = mm_in(*g_state, rest, 2 * DV, DV, scalars, "back_out")
    grad_gate, grad_retained = gate_back(grad_mixed)
    grad_low = grad_retained.reshape(2, rows, DV).astype(BF)
    query_in = (query.astype(F32) * enter).astype(BF)
    state_back = carry(ein("gid,gie->gde", query_in, grad_low), -1).astype(BF)
    grad_scores = (ein("gie,gje->gij", grad_low, value) * mask).astype(BF)
    grad_query = ein("gij,gjd->gid", grad_scores, key) + enter * ein("gie,gde->gid", grad_low, state_in)
    grad_key = ein("gij,gid->gjd", grad_scores, query) + leave * ein("gje,gde->gjd", value, state_back)
    grad_value = ein("gij,gie->gje", weighted, grad_low) + ein("gjd,gde->gje", key_out, state_back)
    grad_proj = jnp.concatenate(
        (
            rotate(grad_query.reshape(2 * rows, DK), cosine, -sine),
            rotate(grad_key.reshape(2 * rows, DK), cosine, -sine),
            grad_value.reshape(2 * rows, DV),
            grad_gate,
        ),
        axis=1,
    ).astype(BF)
    d_attn = mm_weight(((x_first, grad_proj), (g_state, mixed)), scalars, "weight_attn")
    parts = heads_total(*mm_back(grad_proj, attn, 0, scalars, "back_attn"))
    input_grad, gain_first_part = norm_back(
        tokens, grad_state, parts, gain_first, True, scalars, "first_back"
    )

    def scattered(grad):
        block = lax.psum_scatter(
            grad.reshape(16, 128, -1).reshape(2048, -1), XY, scatter_dimension=0, tiled=True
        )
        return block[:64], swap(block[64:])

    d_hidden, d_linear, d_down = join_heads(
        *scattered(d_mlp), (DV, DV, DV), (False, False, True), scalars, "join_mlp"
    )
    d_query, d_key, d_value, d_gate, d_output = join_heads(
        *scattered(d_attn),
        (DK, DK, DV, DV, DV),
        (False, False, False, False, True),
        scalars,
        "join_attn",
    )

    def gain_total(part):
        part = part + swap(part)
        for axis in XY:
            part = part + shift(part, axis, 1) + shift(part, axis, 2) + shift(part, axis, 3)
        spot = (lax.axis_index("x") * 2 + core) * 4 + place
        return lax.dynamic_slice_in_dim(part, spot * 64, 64, 1)

    gains = gain_total(jnp.stack((gain_first_part, gain_second_part)))
    return (
        layer_out,
        input_grad,
        gains[0],
        gains[1],
        d_query,
        d_key,
        d_value,
        d_gate,
        d_output,
        d_hidden,
        d_linear,
        d_down,
    )


def solution(mesh):
    fine = Mesh(np.asarray(mesh.devices).reshape(4, 2, 4, 4), ("x", "core", "ctx", "tp"))
    split = ("x", "core", "ctx")
    row = P(split, None)
    win = P(split, "tp")
    wout = P("tp", split)
    in_specs = (row, row, P(), P(), win, win, win, win, wout, win, win, wout, P("tp"), P(("x", "core")))
    out_specs = (row, row, P(split), P(split), win, win, win, win, wout, win, win, wout)
    return jax.shard_map(
        per_device, mesh=fine, in_specs=in_specs, out_specs=out_specs, check_vma=False
    )
```

time: 527 us -> 512 us (0.972)
  waiting for transfers between devices: 180 us -> 298 us
  local copies, waits for them, and re-layouts: 140 us -> 22.9 us
  Pallas kernels: 0 us -> 80.3 us
  other arithmetic: 64.4 us -> 9.67 us
  matrix products: 48.2 us -> 4.06 us
    pallas_call x0 -> x19, Pallas kernels: none -> 80.3 us  [call(): pl.pallas_call(body, out_shape=shapes, grid_spec=pltpu.PrefetchScalarGrid...]
    reduce_scatter x2, waiting for transfers between devices: 0.02 us -> 74.4 us  [scattered(): lax.psum_scatter(grad.reshape(16, 128, -1).reshape(2048, -1), XY, scatter...]
    concatenate x32 -> x0, local copies, waits for them, and re-layouts: 67 us -> none  [heads_total(): return jnp.concatenate(parts, axis=0).astype(F32)]
    dot_general x12 -> x0, matrix products: 44.1 us -> none  [the longest x4 15.7 us: dot(): return jnp.dot(left, right, preferred_element_type=F32)]
    ppermute x30, waiting for transfers between devices: 38.6 us -> 72.6 us  [shift(): return lax.ppermute(value, axis, [(i, (i + offset) % n) for i in range(n)])]
    unnamed x171 -> x99, local copies, waits for them, and re-layouts: 38.4 us -> 17.3 us
    concatenate x12 -> x3, other arithmetic: 21.5 us -> 1.76 us  [the longest x2 1.64 us: gathered(): block = jnp.concatenate((mine, swap(theirs)), axis=0)]
    reshape x13 -> x0, local copies, waits for them, and re-layouts: 17.7 us -> none  [the longest x5 13.7 us: columns_in(): value.reshape(*lead, 4, 2, 4, 64).swapaxes(-3, -2).reshape(*lead, 2048)]
  transfers between devices with their start and end apart: 54 -> 54, of which waited for: 24 -> 28; matrix products, arithmetic and copies ran while one was open for 42% -> 3% of each run, Pallas kernels for 0% -> 9%
where the time goes in v2:
time: 512 us; the launch traced here: 503 us
  waiting for transfers between devices  298 us (58%)
  Pallas kernels  80.3 us (16%)
  starting transfers between devices  71.2 us (14%)
  local copies, waits for them, and re-layouts  22.9 us (4%)
  between operations  16.5 us (3%)
  other arithmetic  9.67 us (2%)
    all_gather x2, waiting for transfers between devices, gathered(): lax.all_gather(block, XY, axis=0, tiled=True).reshape(4, 4, 2, 64, -1)  89.6 us
    pallas_call x19, Pallas kernels, call(): pl.pallas_call(body, out_shape=shapes, grid_spec=pltpu.PrefetchScalarGrid...  80.3 us
    reduce_scatter x2, waiting for transfers between devices, scattered(): lax.psum_scatter(grad.reshape(16, 128, -1).reshape(2048, -1), XY, scatter...  74.4 us
    ppermute x30, waiting for transfers between devices, shift(): return lax.ppermute(value, axis, [(i, (i + offset) % n) for i in range(n)])  72.6 us
    ppermute x6, waiting for transfers between devices, shift_open(): lax.ppermute(value, axis, [(i, i + offset) for i in range(n) if 0 <= i +...  49.2 us
    ppermute x30, starting transfers between devices, shift(): return lax.ppermute(value, axis, [(i, (i + offset) % n) for i in range(n)])  43.2 us
    unnamed x99, local copies, waits for them, and re-layouts  17.3 us
    ppermute x14, starting transfers between devices, swap(): return lax.ppermute(value, 'core', [(0, 1), (1, 0)])  15.6 us
  transfers between devices with their start and end apart: 54, of which 28 were waited for; matrix products, arithmetic and copies ran while one was open for 3% of the time, Pallas kernels for 9%

profile of v2, /device:TPU:1, one launch (start us, length us, event | category | flops | bytes accessed | tf_op | source)
XLA Modules:
  0.0 502.7 jit_solution(18261933860383529832)
XLA Ops:
  11.4 1.5 collective-permute-start.1
  20.7 4.9 enter_rows.1
  31.4 46.9 %all-gather.3.cloned.1.call-done = bf16[2048,1536]{1,0:T(8,128)(2,1)} async-done(((bf16[128,1536]{1,0:T(8,128)(2,1)}), bf16[2048,1536]{1,0:T(8,128)(2,1)}) %all-gather.3.cloned.1.call-update) | async-done | bytes 6291472 | tf_op jit(solution)/shard_map/all_gather | solution.py:429
  78.3 7.4 %project_attn.1 = f32[512,1536]{1,0:T(8,128)S(1)} custom-call(s32[2]{0:T(128)S(1)} %pad_add_fusion.s_ref, bf16[256,2048]{1,0:T(8,128)(2,1)S(1)} %get-tuple-element.53.a_ref.refs_0_, bf16[256,2048]{1,0:T(8,128)(2,1)} %collective-permute-done.b_ref.refs_1_, bf16[4,4,2,64,1536]{4,3,2,1,0:T(8,128)(2,1)} %bitcast.174), custom_call_target="tpu_custom_call" | custom-call | flops 3221225472 | bytes 11534336 | tf_op jit(solution)/shard_map/project_attn/pallas_call | solution.py:41
  86.4 4.3 collective-permute-start.5
  92.1 2.5 collective-permute-start.3
  95.0 26.7 %collective-permute-done.5 = bf16[2,256,512]{2,1,0:T(8,128)(2,1)S(1)} collective-permute-done((bf16[2,256,512]{2,1,0:T(8,128)(2,1)S(1)}, bf16[2,256,512]{2,1,0:T(8,128)(2,1)S(1)}, u32[]{:S(2)}, u32[]{:S(2)}) %collective-permute-start.5) | collective-permute-done | bytes 524320 | tf_op jit(solution)/shard_map/ppermute | solution.py:26
  124.3 42.6 %all-gather.5.cloned.1.call-done = bf16[2048,2048]{1,0:T(8,128)(2,1)} async-done(((bf16[128,2048]{1,0:T(8,128)(2,1)}), bf16[2048,2048]{1,0:T(8,128)(2,1)}) %all-gather.5.cloned.1.call-update) | async-done | bytes 8388624 | tf_op jit(solution)/shard_map/all_gather | solution.py:429
  166.9 4.2 project_out.1
  171.9 2.3 collective-permute-done.7
  174.4 1.3 collective-permute-start.8
  175.8 2.6 collective-permute-start.10
  179.4 3.8 collective-permute-done.8
  183.2 6.8 %collective-permute-done.10 = bf16[64,2048]{1,0:T(8,128)(2,1)S(1)} collective-permute-done((bf16[64,2048]{1,0:T(8,128)(2,1)S(1)}, bf16[64,2048]{1,0:T(8,128)(2,1)S(1)}, u32[]{:S(2)}, u32[]{:S(2)}) %collective-permute-start.10) | collective-permute-done | bytes 262176 | tf_op jit(solution)/shard_map/ppermute | solution.py:21
  191.2 2.9 collective-permute-start.12
  194.4 2.3 collective-permute-start.22
  196.7 1.4 collective-permute-done.13.refs_3_
  198.1 7.5 %collective-permute-done.12.refs_2_ = bf16[64,2048]{1,0:T(8,128)(2,1)S(1)} collective-permute-done((bf16[64,2048]{1,0:T(8,128)(2,1)S(1)}, bf16[64,2048]{1,0:T(8,128)(2,1)S(1)}, u32[]{:S(2)}, u32[]{:S(2)}) %collective-permute-start.12) | collective-permute-done | bytes 262176 | tf_op jit(solution)/shard_map/ppermute | solution.py:21
  205.6 3.3 second_norm.1
  210.1 1.5 collective-permute-start.14
  211.6 4.4 back_down.1
  216.1 5.8 %project_mlp.1 = f32[512,1024]{1,0:T(8,128)S(1)} custom-call(s32[2]{0:T(128)S(1)} %pad_add_fusion.s_ref, bf16[256,2048]{1,0:T(8,128)(2,1)S(1)} %get-tuple-element.64.a_ref.refs_0_, bf16[256,2048]{1,0:T(8,128)(2,1)S(1)} %collective-permute-done.14.b_ref.refs_1_, bf16[4,4,2,64,2048]{4,3,2,1,0:T(8,128)(2,1)} %bitcast.136), custom_call_target="tpu_custom_call" | custom-call | flops 2147483648 | bytes 12582912 | tf_op jit(solution)/shard_map/project_mlp/pallas_call | solution.py:41
  222.9 5.5 %back_mlp.1 = (f32[256,2048]{1,0:T(8,128)S(1)}, bf16[256,2048]{1,0:T(8,128)(2,1)S(1)}) custom-call(s32[2]{0:T(128)S(1)} %pad_add_fusion.s_ref, bf16[512,1024]{1,0:T(8,128)(2,1)S(1)} %pad_maximum_fusion.g_ref.refs_2_, bf16[4,4,2,64,2048]{4,3,2,1,0:T(8,128)(2,1)} %bitcast.137), custom_call_target="tpu_custom_call" | custom-call | flops 2147483648 | bytes 12582912 | tf_op jit(solution)/shard_map/back_mlp/pallas_call | solution.py:41
  228.5 2.6 collective-permute-done.23
  232.4 2.1 collective-permute-start.26
  235.1 5.3 %collective-permute-done.24 = bf16[64,2048]{1,0:T(8,128)(2,1)S(1)} collective-permute-done((bf16[64,2048]{1,0:T(8,128)(2,1)S(1)}, bf16[64,2048]{1,0:T(8,128)(2,1)S(1)}, u32[]{:S(2)}, u32[]{:S(2)}) %collective-permute-start.24) | collective-permute-done | bytes 262176 | tf_op jit(solution)/shard_map/ppermute | solution.py:21
  240.4 6.0 %collective-permute-done.26 = bf16[64,2048]{1,0:T(8,128)(2,1)S(1)} collective-permute-done((bf16[64,2048]{1,0:T(8,128)(2,1)S(1)}, bf16[64,2048]{1,0:T(8,128)(2,1)S(1)}, u32[]{:S(2)}, u32[]{:S(2)}) %collective-permute-start.26) | collective-permute-done | bytes 262176 | tf_op jit(solution)/shard_map/ppermute | solution.py:21
  246.6 1.7 collective-permute-start.29
  248.3 2.6 collective-permute-start.28
  250.9 4.4 collective-permute-done.29.refs_3_
  255.3 7.2 %collective-permute-done.28.refs_2_ = bf16[64,2048]{1,0:T(8,128)(2,1)S(1)} collective-permute-done((bf16[64,2048]{1,0:T(8,128)(2,1)S(1)}, bf16[64,2048]{1,0:T(8,128)(2,1)S(1)}, u32[]{:S(2)}, u32[]{:S(2)}) %collective-permute-start.28) | collective-permute-done | bytes 262176 | tf_op jit(solution)/shard_map/ppermute | solution.py:21
  262.4 4.2 second_back.1
  268.0 1.3 collective-permute-start.30
  269.3 2.3 collective-permute-done.30.b_ref.refs_4_
  271.6 4.4 back_out.1
  281.9 1.5 collective-permute-start.31
  284.2 22.5 %collective-permute-done.33 = bf16[2,256,512]{2,1,0:T(8,128)(2,1)S(1)} collective-permute-done((bf16[2,256,512]{2,1,0:T(8,128)(2,1)S(1)}, bf16[2,256,512]{2,1,0:T(8,128)(2,1)S(1)}, u32[]{:S(2)}, u32[]{:S(2)}) %collective-permute-start.33) | collective-permute-done | bytes 524320 | tf_op jit(solution)/shard_map/ppermute | solution.py:26
  309.5 8.8 %weight_attn.1 = bf16[4,4,2,64,2048]{4,3,2,1,0:T(8,128)(2,1)} custom-call(s32[2]{0:T(128)S(1)} %pad_add_fusion.s_ref, bf16[256,2048]{1,0:T(8,128)(2,1)S(1)} %copy-done.25, bf16[256,2048]{1,0:T(8,128)(2,1)} %collective-permute-done.b_ref.refs_1_, bf16[512,1536]{1,0:T(8,128)(2,1)} %copy-done.22, bf16[256,2048]{1,0:T(8,128)(2,1)S(1)} %get-tuple-element.72.a_ref.refs_3_, ...), custom_call_target="tpu_custom_call" | custom-call | flops 4294967296 | bytes 14680064 | tf_op jit(solution)/shard_map/weight_attn/pallas_call | solution.py:41
  322.1 6.3 %weight_mlp.1 = bf16[4,4,2,64,1536]{4,3,2,1,0:T(8,128)(2,1)} custom-call(s32[2]{0:T(128)S(1)} %pad_add_fusion.s_ref, bf16[256,2048]{1,0:T(8,128)(2,1)S(1)} %copy-done.9, bf16[256,2048]{1,0:T(8,128)(2,1)S(1)} %copy-done.11, bf16[512,1024]{1,0:T(8,128)(2,1)S(1)} %pad_maximum_fusion.g_ref.refs_2_, bf16[256,2048]{1,0:T(8,128)(2,1)S(1)} %get-tuple-element.68.a_ref.refs_3_, ...), custom_call_target="tpu_custom_call" | custom-call | flops 3221225472 | bytes 12058624 | tf_op jit(solution)/shard_map/weight_mlp/pallas_call | solution.py:41
  328.4 1.4 copy-done.23
  329.9 6.7 %back_attn.1 = (f32[256,2048]{1,0:T(8,128)S(1)}, bf16[256,2048]{1,0:T(8,128)(2,1)S(1)}) custom-call(s32[2]{0:T(128)S(1)} %pad_add_fusion.s_ref, bf16[512,1536]{1,0:T(8,128)(2,1)S(1)} %copy-done.23, bf16[4,4,2,64,1536]{4,3,2,1,0:T(8,128)(2,1)} %bitcast.175), custom_call_target="tpu_custom_call" | custom-call | flops 3221225472 | bytes 11010048 | tf_op jit(solution)/shard_map/back_attn/pallas_call | solution.py:41
  337.8 2.3 collective-permute-done.34
  340.9 2.6 collective-permute-start.37
  343.5 4.6 project_down.1
  349.3 5.8 %collective-permute-done.37 = bf16[64,2048]{1,0:T(8,128)(2,1)S(1)} collective-permute-done((bf16[64,2048]{1,0:T(8,128)(2,1)S(1)}, bf16[64,2048]{1,0:T(8,128)(2,1)S(1)}, u32[]{:S(2)}, u32[]{:S(2)}) %collective-permute-start.37) | collective-permute-done | bytes 262176 | tf_op jit(solution)/shard_map/ppermute | solution.py:21
  355.3 1.5 collective-permute-start.40
  356.8 3.1 collective-permute-start.39
  359.9 4.6 collective-permute-done.40.refs_3_
  364.5 7.1 %collective-permute-done.39.refs_2_ = bf16[64,2048]{1,0:T(8,128)(2,1)S(1)} collective-permute-done((bf16[64,2048]{1,0:T(8,128)(2,1)S(1)}, bf16[64,2048]{1,0:T(8,128)(2,1)S(1)}, u32[]{:S(2)}, u32[]{:S(2)}) %collective-permute-start.39) | collective-permute-done | bytes 262176 | tf_op jit(solution)/shard_map/ppermute | solution.py:21
  371.6 3.3 first_back.1
  376.5 3.0 collective-permute-start.18
  379.6 2.7 collective-permute-start.43
  383.1 2.5 collective-permute-done.16
  386.7 4.8 collective-permute-done.18
  392.6 3.6 collective-permute-start.20
  397.4 2.8 collective-permute-start.46
  400.7 2.1 collective-permute-start.45
  402.8 5.0 collective-permute-done.20.refs_2_
  407.7 2.4 leave_rows.1
  411.3 1.4 collective-permute-start.48
  412.8 74.4 %reduce-scatter.5.cloned.1.call-done = bf16[128,1536]{1,0:T(8,128)(2,1)} async-done(((bf16[2048,1536]{1,0:T(8,128)(2,1)}), bf16[128,1536]{1,0:T(8,128)(2,1)}) %reduce-scatter.5.cloned.1.call-update) | async-done | bytes 393232 | tf_op jit(solution)/shard_map/reduce_scatter | solution.py:531
  488.2 1.8 collective-permute-start.49
  491.1 1.4 join_mlp.1
  493.4 1.5 join_attn.1
  (231 shorter events, 58.4 us)
Async XLA Ops:
  7.2 71.1 %all-gather.3.cloned.1.call-start = ((), (), s32[]{:S(2)}) async-start(), calls=%async_computation.2 | async-start | bytes 6684672 | tf_op jit(solution)/shard_map/all_gather | solution.py:429
  11.4 2.6 collective-permute-start.1
  14.8 152.2 %all-gather.5.cloned.1.call-start = ((), (), s32[]{:S(2)}) async-start(), calls=%async_computation.3 | async-start | bytes 8912896 | tf_op jit(solution)/shard_map/all_gather | solution.py:429
  17.7 1.6 collective-permute-start.6
  20.2 390.0 %reduce-scatter.3.cloned.1.call-start = ((), (), s32[]{:S(2)}) async-start(), calls=%async_computation.4 | async-start | bytes 8912896 | tf_op jit(solution)/shard_map/reduce_scatter | solution.py:531
  20.3 10.5 %collective-permute-start.2 = (s32[1]{0:T(128)}, s32[1]{0:T(128)}, u32[]{:S(2)}, u32[]{:S(2)}) collective-permute-start(s32[1]{0:T(128)} %param.27), channel_id=1, source_target_pairs={{0,16},{16,0},{1,17},{17,1},{2,18},{18,2},{3,19},{19,3},{4,20},{20... | collective-permute-start | bytes 20 | tf_op jit(solution)/shard_map/ppermute | solution.py:32
  26.9 58.8 %copy-start.24 = (bf16[256,2048]{1,0:T(8,128)(2,1)}, bf16[256,2048]{1,0:T(8,128)(2,1)S(1)}, u32[]{:S(2)}) copy-start(bf16[256,2048]{1,0:T(8,128)(2,1)S(1)} %get-tuple-element.53.a_ref.refs_0_) | copy-start | bytes 3145732
  26.9 4.5 collective-permute-start
  29.9 55.9 %copy-start.36 = (f32[256,128]{1,0:T(8,128)}, f32[256,128]{1,0:T(8,128)S(1)}, u32[]{:S(2)}) copy-start(f32[256,128]{1,0:T(8,128)S(1)} %get-tuple-element.132) | copy-start | bytes 393220
  29.9 55.9 %copy-start.38 = (f32[256,128]{1,0:T(8,128)}, f32[256,128]{1,0:T(8,128)S(1)}, u32[]{:S(2)}) copy-start(f32[256,128]{1,0:T(8,128)S(1)} %get-tuple-element.133) | copy-start | bytes 393220
  85.7 37.5 %copy-start.4 = (f32[512,1536]{1,0:T(8,128)}, f32[512,1536]{1,0:T(8,128)S(1)}, u32[]{:S(2)}) copy-start(f32[512,1536]{1,0:T(8,128)S(1)} %project_attn.1) | copy-start | bytes 9437188
  85.8 36.6 %copy-start.28 = (bf16[512,512]{1,0:T(8,128)(2,1)}, bf16[512,512]{1,0:T(8,128)(2,1)S(1)}, u32[]{:S(2)}) copy-start(bf16[512,512]{1,0:T(8,128)(2,1)S(1)} %slice.367) | copy-start | bytes 1572868
  86.0 36.1 %copy-start.32 = (bf16[512,128]{1,0:T(8,128)(2,1)}, bf16[512,128]{1,0:T(8,128)(2,1)S(1)}, u32[]{:S(2)}) copy-start(bf16[512,128]{1,0:T(8,128)(2,1)S(1)} %get-tuple-element.101) | copy-start | bytes 393220
  86.0 36.1 %copy-start.34 = (bf16[512,128]{1,0:T(8,128)(2,1)}, bf16[512,128]{1,0:T(8,128)(2,1)S(1)}, u32[]{:S(2)}) copy-start(bf16[512,128]{1,0:T(8,128)(2,1)S(1)} %get-tuple-element.104) | copy-start | bytes 393220
  86.4 35.3 %collective-permute-start.5 = (bf16[2,256,512]{2,1,0:T(8,128)(2,1)S(1)}, bf16[2,256,512]{2,1,0:T(8,128)(2,1)S(1)}, u32[]{:S(2)}, u32[]{:S(2)}) collective-permute-start(bf16[2,256,512]{2,1,0:T(8,128)(2,1)S(1)} %convolution_convert_fusion.1), channel_id=1, source_target_pairs={{0,12},{1,13},{2,14},{3,15},{16,28},{17,29},{18,30},{19,31},{32,44... | collective-permute-start | bytes 1572872 | tf_op jit(solution)/shard_map/ppermute | solution.py:26
  90.8 31.0 %collective-permute-start.4 = (bf16[2,256,512]{2,1,0:T(8,128)(2,1)S(1)}, bf16[2,256,512]{2,1,0:T(8,128)(2,1)S(1)}, u32[]{:S(2)}, u32[]{:S(2)}) collective-permute-start(bf16[2,256,512]{2,1,0:T(8,128)(2,1)S(1)} %convolution_convert_fusion.1), channel_id=1, source_target_pairs={{0,8},{4,12},{1,9},{5,13},{2,10},{6,14},{3,11},{7,15},{16,24},{20,... | collective-permute-start | bytes 1572872 | tf_op jit(solution)/shard_map/ppermute | solution.py:26
  92.1 29.7 %collective-permute-start.3 = (bf16[2,256,512]{2,1,0:T(8,128)(2,1)S(1)}, bf16[2,256,512]{2,1,0:T(8,128)(2,1)S(1)}, u32[]{:S(2)}, u32[]{:S(2)}) collective-permute-start(bf16[2,256,512]{2,1,0:T(8,128)(2,1)S(1)} %convolution_convert_fusion.1), channel_id=1, source_target_pairs={{0,4},{4,8},{8,12},{1,5},{5,9},{9,13},{2,6},{6,10},{10,14},{3,7},{... | collective-permute-start | bytes 1572872 | tf_op jit(solution)/shard_map/ppermute | solution.py:26
  171.2 3.0 collective-permute-start.7
  174.2 31.4 %copy-start.20 = (f32[2048]{0:T(1024)S(1)}, f32[2048]{0:T(1024)}, u32[]{:S(2)}) copy-start(f32[2048]{0:T(1024)} %param.17) | copy-start | bytes 24580
  174.4 8.8 %collective-permute-start.8 = (bf16[64,2048]{1,0:T(8,128)(2,1)S(1)}, bf16[64,2048]{1,0:T(8,128)(2,1)S(1)}, u32[]{:S(2)}, u32[]{:S(2)}) collective-permute-start(bf16[64,2048]{1,0:T(8,128)(2,1)S(1)} %get-tuple-element.116), channel_id=1, source_target_pairs={{0,1},{1,2},{2,3},{3,0},{4,5},{5,6},{6,7},{7,4},{8,9},{9,10},{10,1... | collective-permute-start | bytes 786440 | tf_op jit(solution)/shard_map/ppermute | solution.py:21
  175.8 14.2 %collective-permute-start.10 = (bf16[64,2048]{1,0:T(8,128)(2,1)S(1)}, bf16[64,2048]{1,0:T(8,128)(2,1)S(1)}, u32[]{:S(2)}, u32[]{:S(2)}) collective-permute-start(bf16[64,2048]{1,0:T(8,128)(2,1)S(1)} %get-tuple-element.117), channel_id=1, source_target_pairs={{0,2},{1,3},{2,0},{3,1},{4,6},{5,7},{6,4},{7,5},{8,10},{9,11},{10,... | collective-permute-start | bytes 786440 | tf_op jit(solution)/shard_map/ppermute | solution.py:21
  178.3 11.7 %collective-permute-start.9 = (bf16[64,2048]{1,0:T(8,128)(2,1)S(1)}, bf16[64,2048]{1,0:T(8,128)(2,1)S(1)}, u32[]{:S(2)}, u32[]{:S(2)}) collective-permute-start(bf16[64,2048]{1,0:T(8,128)(2,1)S(1)} %get-tuple-element.118), channel_id=1, source_target_pairs={{0,3},{1,0},{2,1},{3,2},{4,7},{5,4},{6,5},{7,6},{8,11},{9,8},{10,9... | collective-permute-start | bytes 786440 | tf_op jit(solution)/shard_map/ppermute | solution.py:21
  190.2 7.9 %collective-permute-start.13 = (bf16[64,2048]{1,0:T(8,128)(2,1)S(1)}, bf16[64,2048]{1,0:T(8,128)(2,1)S(1)}, u32[]{:S(2)}, u32[]{:S(2)}) collective-permute-start(bf16[64,2048]{1,0:T(8,128)(2,1)S(1)} %add_convert_fusion.18.refs_0_), channel_id=1, source_target_pairs={{0,1},{1,2},{2,3},{3,0},{4,5},{5,6},{6,7},{7,4},{8,9},{9,10},{10,1... | collective-permute-start | bytes 786440 | tf_op jit(solution)/shard_map/ppermute | solution.py:21
  191.2 14.4 %collective-permute-start.12 = (bf16[64,2048]{1,0:T(8,128)(2,1)S(1)}, bf16[64,2048]{1,0:T(8,128)(2,1)S(1)}, u32[]{:S(2)}, u32[]{:S(2)}) collective-permute-start(bf16[64,2048]{1,0:T(8,128)(2,1)S(1)} %add_convert_fusion.18.refs_0_), channel_id=1, source_target_pairs={{0,2},{1,3},{2,0},{3,1},{4,6},{5,7},{6,4},{7,5},{8,10},{9,11},{10,... | collective-permute-start | bytes 786440 | tf_op jit(solution)/shard_map/ppermute | solution.py:21
  194.0 11.5 %collective-permute-start.11 = (bf16[64,2048]{1,0:T(8,128)(2,1)S(1)}, bf16[64,2048]{1,0:T(8,128)(2,1)S(1)}, u32[]{:S(2)}, u32[]{:S(2)}) collective-permute-start(bf16[64,2048]{1,0:T(8,128)(2,1)S(1)} %add_convert_fusion.18.refs_0_), channel_id=1, source_target_pairs={{0,3},{1,0},{2,1},{3,2},{4,7},{5,4},{6,5},{7,6},{8,11},{9,8},{10,9... | collective-permute-start | bytes 786440 | tf_op jit(solution)/shard_map/ppermute | solution.py:21
  194.4 17.3 %collective-permute-start.22 = (bf16[256,2048]{1,0:T(8,128)(2,1)S(1)}, bf16[256,2048]{1,0:T(8,128)(2,1)S(1)}, u32[]{:S(2)}, u32[]{:S(2)}) collective-permute-start(bf16[256,2048]{1,0:T(8,128)(2,1)S(1)} %get-tuple-element.68.a_ref.refs_3_), channel_id=1, source_target_pairs={{0,16},{16,0},{1,17},{17,1},{2,18},{18,2},{3,19},{19,3},{4,20},{20... | collective-permute-start | bytes 3145736 | tf_op jit(solution)/shard_map/ppermute | solution.py:32
  210.1 5.9 %collective-permute-start.14 = (bf16[256,2048]{1,0:T(8,128)(2,1)S(1)}, bf16[256,2048]{1,0:T(8,128)(2,1)S(1)}, u32[]{:S(2)}, u32[]{:S(2)}) collective-permute-start(bf16[256,2048]{1,0:T(8,128)(2,1)S(1)} %get-tuple-element.64.a_ref.refs_0_), channel_id=1, source_target_pairs={{0,16},{16,0},{1,17},{17,1},{2,18},{18,2},{3,19},{19,3},{4,20},{20... | collective-permute-start | bytes 3145736 | tf_op jit(solution)/shard_map/ppermute | solution.py:32
  228.4 2.7 collective-permute-start.23
  231.4 9.0 %collective-permute-start.24 = (bf16[64,2048]{1,0:T(8,128)(2,1)S(1)}, bf16[64,2048]{1,0:T(8,128)(2,1)S(1)}, u32[]{:S(2)}, u32[]{:S(2)}) collective-permute-start(bf16[64,2048]{1,0:T(8,128)(2,1)S(1)} %get-tuple-element.108), channel_id=1, source_target_pairs={{0,1},{1,2},{2,3},{3,0},{4,5},{5,6},{6,7},{7,4},{8,9},{9,10},{10,1... | collective-permute-start | bytes 786440 | tf_op jit(solution)/shard_map/ppermute | solution.py:21
  232.4 14.1 %collective-permute-start.26 = (bf16[64,2048]{1,0:T(8,128)(2,1)S(1)}, bf16[64,2048]{1,0:T(8,128)(2,1)S(1)}, u32[]{:S(2)}, u32[]{:S(2)}) collective-permute-start(bf16[64,2048]{1,0:T(8,128)(2,1)S(1)} %get-tuple-element.109), channel_id=1, source_target_pairs={{0,2},{1,3},{2,0},{3,1},{4,6},{5,7},{6,4},{7,5},{8,10},{9,11},{10,... | collective-permute-start | bytes 786440 | tf_op jit(solution)/shard_map/ppermute | solution.py:21
  234.5 11.9 %collective-permute-start.25 = (bf16[64,2048]{1,0:T(8,128)(2,1)S(1)}, bf16[64,2048]{1,0:T(8,128)(2,1)S(1)}, u32[]{:S(2)}, u32[]{:S(2)}) collective-permute-start(bf16[64,2048]{1,0:T(8,128)(2,1)S(1)} %get-tuple-element.110), channel_id=1, source_target_pairs={{0,3},{1,0},{2,1},{3,2},{4,7},{5,4},{6,5},{7,6},{8,11},{9,8},{10,9... | collective-permute-start | bytes 786440 | tf_op jit(solution)/shard_map/ppermute | solution.py:21
  246.6 8.7 %collective-permute-start.29 = (bf16[64,2048]{1,0:T(8,128)(2,1)S(1)}, bf16[64,2048]{1,0:T(8,128)(2,1)S(1)}, u32[]{:S(2)}, u32[]{:S(2)}) collective-permute-start(bf16[64,2048]{1,0:T(8,128)(2,1)S(1)} %add_convert_fusion.8.refs_0_), channel_id=1, source_target_pairs={{0,1},{1,2},{2,3},{3,0},{4,5},{5,6},{6,7},{7,4},{8,9},{9,10},{10,1... | collective-permute-start | bytes 786440 | tf_op jit(solution)/shard_map/ppermute | solution.py:21
  248.3 14.1 %collective-permute-start.28 = (bf16[64,2048]{1,0:T(8,128)(2,1)S(1)}, bf16[64,2048]{1,0:T(8,128)(2,1)S(1)}, u32[]{:S(2)}, u32[]{:S(2)}) collective-permute-start(bf16[64,2048]{1,0:T(8,128)(2,1)S(1)} %add_convert_fusion.8.refs_0_), channel_id=1, source_target_pairs={{0,2},{1,3},{2,0},{3,1},{4,6},{5,7},{6,4},{7,5},{8,10},{9,11},{10,... | collective-permute-start | bytes 786440 | tf_op jit(solution)/shard_map/ppermute | solution.py:21
  250.9 11.5 %collective-permute-start.27 = (bf16[64,2048]{1,0:T(8,128)(2,1)S(1)}, bf16[64,2048]{1,0:T(8,128)(2,1)S(1)}, u32[]{:S(2)}, u32[]{:S(2)}) collective-permute-start(bf16[64,2048]{1,0:T(8,128)(2,1)S(1)} %add_convert_fusion.8.refs_0_), channel_id=1, source_target_pairs={{0,3},{1,0},{2,1},{3,2},{4,7},{5,4},{6,5},{7,6},{8,11},{9,8},{10,9... | collective-permute-start | bytes 786440 | tf_op jit(solution)/shard_map/ppermute | solution.py:21
  268.0 3.6 collective-permute-start.30
  279.3 27.5 %collective-permute-start.33 = (bf16[2,256,512]{2,1,0:T(8,128)(2,1)S(1)}, bf16[2,256,512]{2,1,0:T(8,128)(2,1)S(1)}, u32[]{:S(2)}, u32[]{:S(2)}) collective-permute-start(bf16[2,256,512]{2,1,0:T(8,128)(2,1)S(1)} %convolution_convert_fusion), channel_id=1, source_target_pairs={{12,0},{13,1},{14,2},{15,3},{28,16},{29,17},{30,18},{31,19},{44,32... | collective-permute-start | bytes 1572872 | tf_op jit(solution)/shard_map/ppermute | solution.py:26
  280.6 26.2 %collective-permute-start.32 = (bf16[2,256,512]{2,1,0:T(8,128)(2,1)S(1)}, bf16[2,256,512]{2,1,0:T(8,128)(2,1)S(1)}, u32[]{:S(2)}, u32[]{:S(2)}) collective-permute-start(bf16[2,256,512]{2,1,0:T(8,128)(2,1)S(1)} %convolution_convert_fusion), channel_id=1, source_target_pairs={{8,0},{12,4},{9,1},{13,5},{10,2},{14,6},{11,3},{15,7},{24,16},{28,... | collective-permute-start | bytes 1572872 | tf_op jit(solution)/shard_map/ppermute | solution.py:26
  281.9 24.9 %collective-permute-start.31 = (bf16[2,256,512]{2,1,0:T(8,128)(2,1)S(1)}, bf16[2,256,512]{2,1,0:T(8,128)(2,1)S(1)}, u32[]{:S(2)}, u32[]{:S(2)}) collective-permute-start(bf16[2,256,512]{2,1,0:T(8,128)(2,1)S(1)} %convolution_convert_fusion), channel_id=1, source_target_pairs={{4,0},{8,4},{12,8},{5,1},{9,5},{13,9},{6,2},{10,6},{14,10},{7,3},{... | collective-permute-start | bytes 1572872 | tf_op jit(solution)/shard_map/ppermute | solution.py:26
  318.4 168.8 %reduce-scatter.5.cloned.1.call-start = ((), (), s32[]{:S(2)}) async-start(), calls=%async_computation.5 | async-start | bytes 6684672 | tf_op jit(solution)/shard_map/reduce_scatter | solution.py:531
  336.6 3.5 collective-permute-start.34
  340.3 9.1 %collective-permute-start.35 = (bf16[64,2048]{1,0:T(8,128)(2,1)S(1)}, bf16[64,2048]{1,0:T(8,128)(2,1)S(1)}, u32[]{:S(2)}, u32[]{:S(2)}) collective-permute-start(bf16[64,2048]{1,0:T(8,128)(2,1)S(1)} %get-tuple-element.105), channel_id=1, source_target_pairs={{0,1},{1,2},{2,3},{3,0},{4,5},{5,6},{6,7},{7,4},{8,9},{9,10},{10,1... | collective-permute-start | bytes 786440 | tf_op jit(solution)/shard_map/ppermute | solution.py:21
  340.9 14.3 %collective-permute-start.37 = (bf16[64,2048]{1,0:T(8,128)(2,1)S(1)}, bf16[64,2048]{1,0:T(8,128)(2,1)S(1)}, u32[]{:S(2)}, u32[]{:S(2)}) collective-permute-start(bf16[64,2048]{1,0:T(8,128)(2,1)S(1)} %get-tuple-element.106), channel_id=1, source_target_pairs={{0,2},{1,3},{2,0},{3,1},{4,6},{5,7},{6,4},{7,5},{8,10},{9,11},{10,... | collective-permute-start | bytes 786440 | tf_op jit(solution)/shard_map/ppermute | solution.py:21
  343.5 11.7 %collective-permute-start.36 = (bf16[64,2048]{1,0:T(8,128)(2,1)S(1)}, bf16[64,2048]{1,0:T(8,128)(2,1)S(1)}, u32[]{:S(2)}, u32[]{:S(2)}) collective-permute-start(bf16[64,2048]{1,0:T(8,128)(2,1)S(1)} %get-tuple-element.107), channel_id=1, source_target_pairs={{0,3},{1,0},{2,1},{3,2},{4,7},{5,4},{6,5},{7,6},{8,11},{9,8},{10,9... | collective-permute-start | bytes 786440 | tf_op jit(solution)/shard_map/ppermute | solution.py:21
  343.5 28.1 %copy-start.13 = (f32[256,2048]{1,0:T(8,128)S(1)}, f32[256,2048]{1,0:T(8,128)}, u32[]{:S(2)}) copy-start(f32[256,2048]{1,0:T(8,128)} %copy-done.12) | copy-start | bytes 6291460
  348.1 28.1 %collective-permute-start.15 = (bf16[256,2048]{1,0:T(8,128)(2,1)S(1)}, bf16[256,2048]{1,0:T(8,128)(2,1)S(1)}, u32[]{:S(2)}, u32[]{:S(2)}) collective-permute-start(bf16[256,2048]{1,0:T(8,128)(2,1)S(1)} %get-tuple-element.66), channel_id=1, source_target_pairs={{0,16},{16,0},{1,17},{17,1},{2,18},{18,2},{3,19},{19,3},{4,20},{20... | collective-permute-start | bytes 3145736 | tf_op jit(solution)/shard_map/ppermute | solution.py:32
  355.3 9.2 %collective-permute-start.40 = (bf16[64,2048]{1,0:T(8,128)(2,1)S(1)}, bf16[64,2048]{1,0:T(8,128)(2,1)S(1)}, u32[]{:S(2)}, u32[]{:S(2)}) collective-permute-start(bf16[64,2048]{1,0:T(8,128)(2,1)S(1)} %add_convert_fusion.3.refs_0_), channel_id=1, source_target_pairs={{0,1},{1,2},{2,3},{3,0},{4,5},{5,6},{6,7},{7,4},{8,9},{9,10},{10,1... | collective-permute-start | bytes 786440 | tf_op jit(solution)/shard_map/ppermute | solution.py:21
  356.8 14.8 %collective-permute-start.39 = (bf16[64,2048]{1,0:T(8,128)(2,1)S(1)}, bf16[64,2048]{1,0:T(8,128)(2,1)S(1)}, u32[]{:S(2)}, u32[]{:S(2)}) collective-permute-start(bf16[64,2048]{1,0:T(8,128)(2,1)S(1)} %add_convert_fusion.3.refs_0_), channel_id=1, source_target_pairs={{0,2},{1,3},{2,0},{3,1},{4,6},{5,7},{6,4},{7,5},{8,10},{9,11},{10,... | collective-permute-start | bytes 786440 | tf_op jit(solution)/shard_map/ppermute | solution.py:21
  359.9 11.7 %collective-permute-start.38 = (bf16[64,2048]{1,0:T(8,128)(2,1)S(1)}, bf16[64,2048]{1,0:T(8,128)(2,1)S(1)}, u32[]{:S(2)}, u32[]{:S(2)}) collective-permute-start(bf16[64,2048]{1,0:T(8,128)(2,1)S(1)} %add_convert_fusion.3.refs_0_), channel_id=1, source_target_pairs={{0,3},{1,0},{2,1},{3,2},{4,7},{5,4},{6,5},{7,6},{8,11},{9,8},{10,9... | collective-permute-start | bytes 786440 | tf_op jit(solution)/shard_map/ppermute | solution.py:21
  374.9 4.6 collective-permute-start.41
  376.2 31.5 %copy-start.3 = (f32[256,2048]{1,0:T(8,128)S(1)}, f32[256,2048]{1,0:T(8,128)}, u32[]{:S(2)}) copy-start(f32[256,2048]{1,0:T(8,128)} %copy-done.2) | copy-start | bytes 6291460
  376.4 9.2 %collective-permute-start.16 = (bf16[64,2048]{1,0:T(8,128)(2,1)S(1)}, bf16[64,2048]{1,0:T(8,128)(2,1)S(1)}, u32[]{:S(2)}, u32[]{:S(2)}) collective-permute-start(bf16[64,2048]{1,0:T(8,128)(2,1)S(1)} %get-tuple-element.113), channel_id=1, source_target_pairs={{0,1},{1,2},{2,3},{3,0},{4,5},{5,6},{6,7},{7,4},{8,9},{9,10},{10,1... | collective-permute-start | bytes 786440 | tf_op jit(solution)/shard_map/ppermute | solution.py:21
  376.5 15.0 %collective-permute-start.18 = (bf16[64,2048]{1,0:T(8,128)(2,1)S(1)}, bf16[64,2048]{1,0:T(8,128)(2,1)S(1)}, u32[]{:S(2)}, u32[]{:S(2)}) collective-permute-start(bf16[64,2048]{1,0:T(8,128)(2,1)S(1)} %get-tuple-element.114), channel_id=1, source_target_pairs={{0,2},{1,3},{2,0},{3,1},{4,6},{5,7},{6,4},{7,5},{8,10},{9,11},{10,... | collective-permute-start | bytes 786440 | tf_op jit(solution)/shard_map/ppermute | solution.py:21
  379.5 12.1 %collective-permute-start.17 = (bf16[64,2048]{1,0:T(8,128)(2,1)S(1)}, bf16[64,2048]{1,0:T(8,128)(2,1)S(1)}, u32[]{:S(2)}, u32[]{:S(2)}) collective-permute-start(bf16[64,2048]{1,0:T(8,128)(2,1)S(1)} %get-tuple-element.115), channel_id=1, source_target_pairs={{0,3},{1,0},{2,1},{3,2},{4,7},{5,4},{6,5},{7,6},{8,11},{9,8},{10,9... | collective-permute-start | bytes 786440 | tf_op jit(solution)/shard_map/ppermute | solution.py:21
  379.6 16.6 %collective-permute-start.43 = (f32[2,2048]{1,0:T(2,128)S(1)}, f32[2,2048]{1,0:T(2,128)S(1)}, u32[]{:S(2)}, u32[]{:S(2)}) collective-permute-start(f32[2,2048]{1,0:T(2,128)S(1)} %fusion.43), channel_id=1, source_target_pairs={{0,64},{32,96},{64,0},{96,32},{1,65},{33,97},{65,1},{97,33},{2,66}... | collective-permute-start | bytes 49160 | tf_op jit(solution)/shard_map/ppermute | solution.py:21
  382.2 14.0 %collective-permute-start.44 = (f32[2,2048]{1,0:T(2,128)S(1)}, f32[2,2048]{1,0:T(2,128)S(1)}, u32[]{:S(2)}, u32[]{:S(2)}) collective-permute-start(f32[2,2048]{1,0:T(2,128)S(1)} %fusion.43), channel_id=1, source_target_pairs={{0,96},{32,0},{64,32},{96,64},{1,97},{33,1},{65,33},{97,65},{2,98}... | collective-permute-start | bytes 49160 | tf_op jit(solution)/shard_map/ppermute | solution.py:21
  385.6 10.6 %collective-permute-start.42 = (f32[2,2048]{1,0:T(2,128)S(1)}, f32[2,2048]{1,0:T(2,128)S(1)}, u32[]{:S(2)}, u32[]{:S(2)}) collective-permute-start(f32[2,2048]{1,0:T(2,128)S(1)} %fusion.43), channel_id=1, source_target_pairs={{0,32},{32,64},{64,96},{96,0},{1,33},{33,65},{65,97},{97,1},{2,34}... | collective-permute-start | bytes 49160 | tf_op jit(solution)/shard_map/ppermute | solution.py:21
  391.8 8.9 %collective-permute-start.21 = (bf16[64,2048]{1,0:T(8,128)(2,1)S(1)}, bf16[64,2048]{1,0:T(8,128)(2,1)S(1)}, u32[]{:S(2)}, u32[]{:S(2)}) collective-permute-start(bf16[64,2048]{1,0:T(8,128)(2,1)S(1)} %add_convert_fusion.13.refs_0_), channel_id=1, source_target_pairs={{0,1},{1,2},{2,3},{3,0},{4,5},{5,6},{6,7},{7,4},{8,9},{9,10},{10,1... | collective-permute-start | bytes 786440 | tf_op jit(solution)/shard_map/ppermute | solution.py:21
  392.6 15.1 %collective-permute-start.20 = (bf16[64,2048]{1,0:T(8,128)(2,1)S(1)}, bf16[64,2048]{1,0:T(8,128)(2,1)S(1)}, u32[]{:S(2)}, u32[]{:S(2)}) collective-permute-start(bf16[64,2048]{1,0:T(8,128)(2,1)S(1)} %add_convert_fusion.13.refs_0_), channel_id=1, source_target_pairs={{0,2},{1,3},{2,0},{3,1},{4,6},{5,7},{6,4},{7,5},{8,10},{9,11},{10,... | collective-permute-start | bytes 786440 | tf_op jit(solution)/shard_map/ppermute | solution.py:21
  396.2 11.5 %collective-permute-start.19 = (bf16[64,2048]{1,0:T(8,128)(2,1)S(1)}, bf16[64,2048]{1,0:T(8,128)(2,1)S(1)}, u32[]{:S(2)}, u32[]{:S(2)}) collective-permute-start(bf16[64,2048]{1,0:T(8,128)(2,1)S(1)} %add_convert_fusion.13.refs_0_), channel_id=1, source_target_pairs={{0,3},{1,0},{2,1},{3,2},{4,7},{5,4},{6,5},{7,6},{8,11},{9,8},{10,9... | collective-permute-start | bytes 786440 | tf_op jit(solution)/shard_map/ppermute | solution.py:21
  396.2 13.9 %collective-permute-start.47 = (f32[2,2048]{1,0:T(2,128)S(1)}, f32[2,2048]{1,0:T(2,128)S(1)}, u32[]{:S(2)}, u32[]{:S(2)}) collective-permute-start(f32[2,2048]{1,0:T(2,128)S(1)} %add_add_fusion.1), channel_id=1, source_target_pairs={{0,12},{4,0},{8,4},{12,8},{1,13},{5,1},{9,5},{13,9},{2,14},{6,2},{... | collective-permute-start | bytes 49160 | tf_op jit(solution)/shard_map/ppermute | solution.py:21
  397.4 12.8 %collective-permute-start.46 = (f32[2,2048]{1,0:T(2,128)S(1)}, f32[2,2048]{1,0:T(2,128)S(1)}, u32[]{:S(2)}, u32[]{:S(2)}) collective-permute-start(f32[2,2048]{1,0:T(2,128)S(1)} %add_add_fusion.1), channel_id=1, source_target_pairs={{0,8},{4,12},{8,0},{12,4},{1,9},{5,13},{9,1},{13,5},{2,10},{6,14},... | collective-permute-start | bytes 49160 | tf_op jit(solution)/shard_map/ppermute | solution.py:21
  400.7 9.5 %collective-permute-start.45 = (f32[2,2048]{1,0:T(2,128)S(1)}, f32[2,2048]{1,0:T(2,128)S(1)}, u32[]{:S(2)}, u32[]{:S(2)}) collective-permute-start(f32[2,2048]{1,0:T(2,128)S(1)} %add_add_fusion.1), channel_id=1, source_target_pairs={{0,4},{4,8},{8,12},{12,0},{1,5},{5,9},{9,13},{13,1},{2,6},{6,10},{... | collective-permute-start | bytes 49160 | tf_op jit(solution)/shard_map/ppermute | solution.py:21
  411.3 82.0 %collective-permute-start.48 = (bf16[64,2048]{1,0:T(8,128)(2,1)S(1)}, bf16[64,2048]{1,0:T(8,128)(2,1)S(1)}, u32[]{:S(2)}, u32[]{:S(2)}) collective-permute-start(bf16[64,2048]{1,0:T(8,128)(2,1)S(1)} %get-tuple-element.124), channel_id=1, source_target_pairs={{0,16},{16,0},{1,17},{17,1},{2,18},{18,2},{3,19},{19,3},{4,20},{20... | collective-permute-start | bytes 786440 | tf_op jit(solution)/shard_map/ppermute | solution.py:32
  488.2 2.9 collective-permute-start.49
  (35 other events, 152.1 us)
Sparse Core Ops, SparseCore 0:
  14.9 63.3 all-gather.2
  80.4 86.4 all-gather.4
  318.5 84.0 reduce-scatter.2
  405.8 81.2 reduce-scatter.4
